TPU v7x, 32 devices: a whole 2x2x4 slice. The times are simulated.
32 devices in a mesh: grp: 4 (over y, x), tok: 8 (over z, core).
Axes of the slice: x: 2, y: 2, z: 4, core: 2. Of those that a mesh axis runs over, the one named last changes fastest.
Arguments:
- tokens_in: bfloat16 [32768, 768], P(('grp', 'tok')), may hold values from -6 to 6
- w_qkv: bfloat16 [768, 2304], replicated, may hold values from -0.3125 to 0.3125
- b_query: bfloat16 [768], replicated, may hold values from -3 to 3
- b_value: bfloat16 [768], replicated, may hold values from -3 to 3
- w_out: bfloat16 [768, 768], replicated, may hold values from -0.875 to 0.875
- b_out: bfloat16 [768], replicated, may hold values from -3 to 3
- norm1_gain: bfloat16 [768], replicated, may hold values from 0.5 to 1.5
- norm1_shift: bfloat16 [768], replicated, may hold values from -2 to 2
- w_up: bfloat16 [768, 3072], replicated, may hold values from -0.21875 to 0.21875
- b_up: bfloat16 [3072], replicated, may hold values from -3 to 3
- w_down: bfloat16 [3072, 768], replicated, may hold values from -0.109375 to 0.109375
- b_down: bfloat16 [768], replicated, may hold values from -3 to 3
- norm2_gain: bfloat16 [768], replicated, may hold values from 0.5 to 1.5
- norm2_shift: bfloat16 [768], replicated, may hold values from -2 to 2
- out_grad: bfloat16 [32768, 768], P(('grp', 'tok')), may hold values from -6 to 6
- doc_lengths: int32 [4, 5], P('grp'), may hold values from 1 to 7680, as said below
- cluster_slots: int32 [32768], P(('grp', 'tok')), may hold values from 0 to 8191, as said below
Outputs:
- block_out: bfloat16 [32768, 768], P(('grp', 'tok'))
- grad_tokens: bfloat16 [32768, 768], P(('grp', 'tok'))
- grad_w_qkv: float32 [768, 2304], P('tok')
- grad_b_query: float32 [768], P('tok')
- grad_b_value: float32 [768], P('tok')
- grad_w_out: float32 [768, 768], P('tok')
- grad_b_out: float32 [768], P('tok')
- grad_norm1_gain: float32 [768], P('tok')
- grad_norm1_shift: float32 [768], P('tok')
- grad_w_up: float32 [768, 3072], P('tok')
- grad_b_up: float32 [3072], P('tok')
- grad_w_down: float32 [3072, 768], P('tok')
- grad_b_down: float32 [768], P('tok')
- grad_norm2_gain: float32 [768], P('tok')
- grad_norm2_shift: float32 [768], P('tok')
Inputs may be any that keep to these rules, and one draw needn't show every extreme that they name: `doc_lengths`: in each group the documents, each padded up to a multiple of 128 rows, fill the group's rows exactly; one document of each group has the full length and spans from the group's first device to its last. `cluster_slots`: within each group the slots are a permutation of 0 to the group's rows - 1; the rows of every device of a group go to the slot range s // 1024 of every device of the group in equal numbers, 1024 / 8 each.
All inputs are finite; a program needn't handle non-finite values.
Results may differ from a plain program's by a relative error of at most 0.017.
The roundings to bfloat16 on the way count: a program that leaves them out, or rounds other values in their place, can miss the bound.
Values may be sent and summed in bfloat16 or wider, within the bound.
A program may use at most 192 MiB of HBM per device.

v0:
```python
import jax
import jax.numpy as jnp
from jax import lax
from jax.sharding import PartitionSpec as P

H = 12
CLU = 128


eps = 1e-12
masked_score = -1000000000.0


def norm_rows(values, scales, shifts):
    centre = values - jnp.mean(values, axis=-1, keepdims=True)
    spread = jnp.mean(centre * centre, axis=-1, keepdims=True)
    return centre * lax.rsqrt(spread + eps) * scales + shifts


def gelu_exact(values):
    return jax.nn.gelu(values, approximate=False)


def valid_tokens(lengths_row, offset, amount, cluster):
    padded = (lengths_row + cluster - 1) // cluster * cluster
    starts = jnp.cumsum(padded) - padded
    position = offset + jnp.arange(amount, dtype=jnp.int32)
    inside = (position[:, None] >= starts[None, :]) & (
        position[:, None] < (starts + lengths_row)[None, :]
    )
    return jnp.any(inside, axis=1)


def cluster_scores(query, key_rows, live_keys):
    score_scale = query.shape[-1] ** (-0.5)
    scores = (
        jnp.einsum("bqhd,bkhd->bhqk", query, key_rows, preferred_element_type=jnp.float32)
        * score_scale
    )
    return jnp.where(live_keys[:, None, None, :], scores, masked_score)


def cluster_forward(pieces):
    packed, live_keys = pieces
    scores = cluster_scores(packed[:, :, 0], packed[:, :, 1], live_keys)
    top = jnp.max(scores, axis=-1, keepdims=True)
    expo = jnp.exp(scores - top)
    total = jnp.sum(expo, axis=-1, keepdims=True)
    attn_weights = (expo / total).astype(jnp.bfloat16)
    context = jnp.einsum(
        "bhqk,bkhd->bqhd", attn_weights, packed[:, :, 2], preferred_element_type=jnp.float32
    )
    return (context.astype(jnp.bfloat16), top + jnp.log(total))


def cluster_backward(pieces):
    packed, live_keys, log_total, grad_context = pieces
    query = packed[:, :, 0]
    key_rows = packed[:, :, 1]
    value = packed[:, :, 2]
    score_scale = query.shape[-1] ** (-0.5)
    probs_full = jnp.exp(cluster_scores(query, key_rows, live_keys) - log_total)
    grad_probs = jnp.einsum(
        "bqhd,bkhd->bhqk", grad_context, value, preferred_element_type=jnp.float32
    )
    row_dot = jnp.sum(grad_probs * probs_full, axis=-1, keepdims=True)
    grad_scores = (probs_full * (grad_probs - row_dot)).astype(jnp.bfloat16)
    grad_query = (
        jnp.einsum("bhqk,bkhd->bqhd", grad_scores, key_rows, preferred_element_type=jnp.float32)
        * score_scale
    )
    grad_key = (
        jnp.einsum("bhqk,bqhd->bkhd", grad_scores, query, preferred_element_type=jnp.float32)
        * score_scale
    )
    grad_value = jnp.einsum(
        "bhqk,bqhd->bkhd",
        probs_full.astype(jnp.bfloat16),
        grad_context,
        preferred_element_type=jnp.float32,
    )
    return jnp.stack([grad_query, grad_key, grad_value], axis=2).astype(jnp.bfloat16)


def per_device(
    tokens_in,
    w_qkv,
    b_query,
    b_value,
    w_out,
    b_out,
    norm1_gain,
    norm1_shift,
    w_up,
    b_up,
    w_down,
    b_down,
    norm2_gain,
    norm2_shift,
    out_grad,
    doc_lengths,
    cluster_slots,
):
    tok_dev, model_width = tokens_in.shape
    head_count = H
    head_size = model_width // head_count
    cluster = CLU
    my_index = lax.axis_index("tok")
    usable = valid_tokens(doc_lengths[0], my_index * tok_dev, tok_dev, cluster)
    sort_order = jnp.argsort(cluster_slots)
    undo_order = jnp.argsort(sort_order)
    sent_slots = cluster_slots[sort_order]
    sent_live = usable[sort_order].astype(jnp.int32)
    bias_qkv = jnp.concatenate(
        [
            b_query.astype(jnp.float32),
            jnp.zeros((model_width,), jnp.float32),
            b_value.astype(jnp.float32),
        ]
    )
    qkv_rows = (jnp.dot(tokens_in, w_qkv, preferred_element_type=jnp.float32) + bias_qkv).astype(
        jnp.bfloat16
    )
    got_rows, got_slots, got_live = (
        lax.all_to_all(qkv_rows[sort_order], "tok", split_axis=0, concat_axis=0, tiled=True),
        lax.all_to_all(sent_slots, "tok", split_axis=0, concat_axis=0, tiled=True),
        lax.all_to_all(sent_live, "tok", split_axis=0, concat_axis=0, tiled=True),
    )
    local_pos = got_slots - my_index * tok_dev
    placing = jnp.argsort(local_pos)
    key_live = got_live[placing] > 0
    cluster_qkv = got_rows[placing]
    clusters = tok_dev // cluster
    per_step = min(512 // cluster, clusters)
    step_count = clusters // per_step
    packed_all = cluster_qkv.reshape(step_count, per_step, cluster, 3, head_count, head_size)
    live_all = key_live.reshape(step_count, per_step, cluster)
    context_c, log_total = lax.map(cluster_forward, (packed_all, live_all))
    context_c = context_c.reshape(tok_dev, model_width)
    returned = lax.all_to_all(context_c[local_pos], "tok", split_axis=0, concat_axis=0, tiled=True)
    context_tok = returned[undo_order]
    attn_out = jnp.dot(context_tok, w_out, preferred_element_type=jnp.float32) + b_out.astype(
        jnp.float32
    )
    resid1 = tokens_in.astype(jnp.float32) + attn_out
    normed1, norm1_back = jax.vjp(
        norm_rows, resid1, norm1_gain.astype(jnp.float32), norm1_shift.astype(jnp.float32)
    )
    normed1_low = normed1.astype(jnp.bfloat16)
    up_pre = jnp.dot(normed1_low, w_up, preferred_element_type=jnp.float32) + b_up.astype(
        jnp.float32
    )
    gelu_out, gelu_back = jax.vjp(gelu_exact, up_pre)
    gelu_low = gelu_out.astype(jnp.bfloat16)
    down_out = jnp.dot(gelu_low, w_down, preferred_element_type=jnp.float32) + b_down.astype(
        jnp.float32
    )
    normed2, norm2_back = jax.vjp(
        norm_rows,
        normed1 + down_out,
        norm2_gain.astype(jnp.float32),
        norm2_shift.astype(jnp.float32),
    )
    block_out = normed2.astype(jnp.bfloat16)
    grad_resid2, grad_gain2, grad_shift2 = norm2_back(out_grad.astype(jnp.float32))
    grad_down = grad_resid2.astype(jnp.bfloat16)
    grad_b_down = jnp.sum(grad_down.astype(jnp.float32), axis=0)
    grad_w_down = jnp.einsum("nf,nd->fd", gelu_low, grad_down, preferred_element_type=jnp.float32)
    grad_gelu = jnp.einsum("nd,fd->nf", grad_down, w_down, preferred_element_type=jnp.float32)
    grad_up = gelu_back(grad_gelu)[0].astype(jnp.bfloat16)
    grad_b_up = jnp.sum(grad_up.astype(jnp.float32), axis=0)
    grad_w_up = jnp.einsum("nd,nf->df", normed1_low, grad_up, preferred_element_type=jnp.float32)
    grad_normed1 = grad_resid2 + jnp.einsum(
        "nf,df->nd", grad_up, w_up, preferred_element_type=jnp.float32
    )
    grad_resid1, grad_gain1, grad_shift1 = norm1_back(grad_normed1)
    grad_attn = grad_resid1.astype(jnp.bfloat16)
    grad_b_out = jnp.sum(grad_attn.astype(jnp.float32), axis=0)
    grad_w_out = jnp.einsum("nd,ne->de", context_tok, grad_attn, preferred_element_type=jnp.float32)
    grad_context = jnp.einsum(
        "ne,de->nd", grad_attn, w_out, preferred_element_type=jnp.float32
    ).astype(jnp.bfloat16)
    grad_context_c = lax.all_to_all(
        grad_context[sort_order], "tok", split_axis=0, concat_axis=0, tiled=True
    )[placing]
    grad_all = grad_context_c.reshape(step_count, per_step, cluster, head_count, head_size)
    grad_qkv_c = lax.map(cluster_backward, (packed_all, live_all, log_total, grad_all))
    grad_qkv_c = grad_qkv_c.reshape(tok_dev, 3 * model_width)
    grad_qkv_tok = lax.all_to_all(
        grad_qkv_c[local_pos], "tok", split_axis=0, concat_axis=0, tiled=True
    )[undo_order]
    grad_w_qkv = jnp.einsum(
        "nd,ne->de", tokens_in, grad_qkv_tok, preferred_element_type=jnp.float32
    )
    grad_qkv_sum = jnp.sum(grad_qkv_tok.astype(jnp.float32), axis=0)
    grad_total = grad_resid1 + jnp.einsum(
        "ne,de->nd", grad_qkv_tok, w_qkv, preferred_element_type=jnp.float32
    )
    grad_tokens = grad_total.astype(jnp.bfloat16)
    grad_b_query = grad_qkv_sum[:model_width]
    grad_b_value = grad_qkv_sum[2 * model_width :]
    all_shares = (
        lax.psum_scatter(grad_w_qkv, "tok", scatter_dimension=0, tiled=True),
        lax.psum_scatter(grad_b_query, "tok", scatter_dimension=0, tiled=True),
        lax.psum_scatter(grad_b_value, "tok", scatter_dimension=0, tiled=True),
        lax.psum_scatter(grad_w_out, "tok", scatter_dimension=0, tiled=True),
        lax.psum_scatter(grad_b_out, "tok", scatter_dimension=0, tiled=True),
        lax.psum_scatter(grad_gain1, "tok", scatter_dimension=0, tiled=True),
        lax.psum_scatter(grad_shift1, "tok", scatter_dimension=0, tiled=True),
        lax.psum_scatter(grad_w_up, "tok", scatter_dimension=0, tiled=True),
        lax.psum_scatter(grad_b_up, "tok", scatter_dimension=0, tiled=True),
        lax.psum_scatter(grad_w_down, "tok", scatter_dimension=0, tiled=True),
        lax.psum_scatter(grad_b_down, "tok", scatter_dimension=0, tiled=True),
        lax.psum_scatter(grad_gain2, "tok", scatter_dimension=0, tiled=True),
        lax.psum_scatter(grad_shift2, "tok", scatter_dimension=0, tiled=True),
    )
    totals = (
        lax.psum(all_shares[0].astype(jnp.bfloat16), "grp").astype(jnp.float32),
        lax.psum(all_shares[1].astype(jnp.bfloat16), "grp").astype(jnp.float32),
        lax.psum(all_shares[2].astype(jnp.bfloat16), "grp").astype(jnp.float32),
        lax.psum(all_shares[3].astype(jnp.bfloat16), "grp").astype(jnp.float32),
        lax.psum(all_shares[4].astype(jnp.bfloat16), "grp").astype(jnp.float32),
        lax.psum(all_shares[5].astype(jnp.bfloat16), "grp").astype(jnp.float32),
        lax.psum(all_shares[6].astype(jnp.bfloat16), "grp").astype(jnp.float32),
        lax.psum(all_shares[7].astype(jnp.bfloat16), "grp").astype(jnp.float32),
        lax.psum(all_shares[8].astype(jnp.bfloat16), "grp").astype(jnp.float32),
        lax.psum(all_shares[9].astype(jnp.bfloat16), "grp").astype(jnp.float32),
        lax.psum(all_shares[10].astype(jnp.bfloat16), "grp").astype(jnp.float32),
        lax.psum(all_shares[11].astype(jnp.bfloat16), "grp").astype(jnp.float32),
        lax.psum(all_shares[12].astype(jnp.bfloat16), "grp").astype(jnp.float32),
    )
    return (
        block_out,
        grad_tokens,
        totals[0],
        totals[1],
        totals[2],
        totals[3],
        totals[4],
        totals[5],
        totals[6],
        totals[7],
        totals[8],
        totals[9],
        totals[10],
        totals[11],
        totals[12],
    )


def solution(mesh):
    in_specs = (
        P(("grp", "tok"), None),
        P(),
        P(),
        P(),
        P(),
        P(),
        P(),
        P(),
        P(),
        P(),
        P(),
        P(),
        P(),
        P(),
        P(("grp", "tok"), None),
        P("grp", None),
        P(("grp", "tok")),
    )
    out_specs = (
        P(("grp", "tok"), None),
        P(("grp", "tok"), None),
        P("tok", None),
        P("tok"),
        P("tok"),
        P("tok", None),
        P("tok"),
        P("tok"),
        P("tok"),
        P("tok", None),
        P("tok"),
        P("tok", None),
        P("tok"),
        P("tok"),
        P("tok"),
    )
    return jax.shard_map(
        per_device, mesh=mesh, in_specs=in_specs, out_specs=out_specs, check_vma=False
    )
```

profile of v0, /device:TPU:0, one launch (start us, length us, event | category | flops | bytes accessed | tf_op | source)
XLA Modules:
  0.0 933.5 jit_solution(5275902657840446558)
XLA Ops:
  7.2 5.2 sort.45
  12.4 10.4 %gather_fusion.1 = s32[1024]{0:T(1024)} fusion(s32[1024]{0:T(1024)} %param.37, s32[1024]{0:T(1024)S(1)} %fusion.31), kind=kCustom, calls=%fused_computation.1 | custom fusion | bytes 12288 | tf_op jit(solution)/shard_map/gather | solution.py:112
  22.8 6.3 all-to-all-start.1
  35.6 6.8 gather_fusion.3
  43.0 5.1 all-to-all-start.2
  48.1 7.4 add_convert_fusion.1
  55.5 12.8 %gather_fusion = bf16[1024,2304]{1,0:T(8,128)(2,1)} fusion(bf16[1024,2304]{1,0:T(8,128)(2,1)} %add_convert_fusion.1, s32[1024]{0:T(1024)S(1)} %fusion.31), kind=kCustom, calls=%fused_computation | custom fusion | bytes 9441280 | tf_op jit(solution)/shard_map/gather | solution.py:125
  68.3 5.6 all-to-all-start
  74.0 4.4 sort.46
  79.1 4.5 gather_fusion.4
  84.2 95.0 %all-to-all-done = bf16[8,128,2304]{2,1,0:T(8,128)(2,1)} async-done(((bf16[8,128,2304]{2,1,0:T(8,128)(2,1)}), bf16[8,128,2304]{2,1,0:T(8,128)(2,1)}, u32[]{:S(2)}, u32[]{:S(2)}) %all-to-all-start) | async-done | bytes 4718624 | tf_op jit(solution)/shard_map/all_to_all | solution.py:125
  179.2 12.8 %gather_fusion.2 = bf16[1024,2304]{1,0:T(8,128)(2,1)} fusion(bf16[1024,2304]{1,0:T(8,128)(2,1)} %bitcast.22, s32[1024]{0:T(1024)S(1)} %fusion.32), kind=kCustom, calls=%fused_computation.2 | custom fusion | bytes 9441280 | tf_op jit(solution)/shard_map/gather | solution.py:132
  192.1 6.6 copy.98
  198.7 8.8 reshape.285
  207.5 5.8 copy.100
  213.2 15.0 %while.22 = (s32[]{:T(128)}, bf16[2,4,128,12,64]{2,1,0,4,3:T(4,128)(2,1)}, f32[2,4,12,128,1]{3,2,1,4,0:T(8,128)}, bf16[2,4,128,3,12,64]{2,5,4,1,3,0:T(8,128)(2,1)}, pred[2,4,128]{2,1,0:T(4,128)(4,1)S(1)}, /*index=5*/s32[]{:T(128)}) while((s32[]{:T(128)}, bf16[2,4,128,12,64]{2,1,0,4,3:T(4,128)(2,1)}, f32[2,4,12,128,1]{3,2,1,4,0:T(8,128)}, ...), condition=%wide.region_7.8_spmd, body=%wide.region_4.7_spmd.sunk | while | flops 211150848 | bytes 32090828 | solution.py:138
  228.2 3.8 reshape.286
  232.0 2.6 copy.102
  234.6 7.2 gather_fusion.5
  241.8 4.3 all-to-all-start.3
  246.1 2.6 copy.95
  248.7 2.6 copy.103
  253.2 4.4 sort.47
  262.2 21.7 %all-to-all-done.3 = bf16[8,128,768]{2,1,0:T(8,128)(2,1)} async-done(((bf16[8,128,768]{2,1,0:T(8,128)(2,1)}), bf16[8,128,768]{2,1,0:T(8,128)(2,1)}, u32[]{:S(2)}, u32[]{:S(2)}) %all-to-all-start.3) | async-done | bytes 1572896 | tf_op jit(solution)/shard_map/all_to_all | solution.py:140
  283.9 7.2 gather_fusion.6
  291.1 4.0 fusion.45
  295.9 37.8 %multiply_convert_fusion.3 = (bf16[1024,3072]{1,0:T(8,128)(2,1)S(1)}, f32[1024,3072]{1,0:T(8,128)}, f32[1024,3072]{1,0:T(8,128)}) fusion(f32[3072]{0:T(1024)S(1)} %copy-done.29, bf16[768,3072]{1,0:T(8,128)(2,1)} %param.29, f32[1024,768]{0,1:T(8,128)S(1)} %get-tuple-element.260, f32[768]{0:T(1024)S(1)} %copy-done.31, f32[768]{0:T(1024)S(1)} %convert_element_type.193, ...), kind=kOutput, calls=%fused_computation.56 | convolution fusion | flops 5043388416 | bytes 39348224 | tf_op jit(solution)/shard_map/dot_general | solution.py:150
  333.8 6.0 fusion.46
  341.5 2.2 fusion.29
  343.8 3.6 convert_reduce_fusion.3
  347.4 17.6 %convert_reduce_fusion = (f32[3072]{0:T(1024)}, bf16[1024,3072]{1,0:T(8,128)(2,1)}) fusion(f32[1024,3072]{1,0:T(8,128)} %get-tuple-element.247, bf16[1024,768]{0,1:T(8,128)(2,1)} %get-tuple-element.241, bf16[3072,768]{1,0:T(8,128)(2,1)} %param.31, f32[1024,3072]{1,0:T(8,128)} %get-tuple-element.261, f32[3072]{0:T(1024)} %convert_element_type.196), kind=kOutput, calls=%fused_computation.54 | convolution fusion | flops 4885312512 | bytes 37773312 | tf_op jit(solution)/shard_map/nd,fd->nf/dot_general | solution.py:169
  365.0 12.1 %multiply_reduce_fusion.1 = (f32[768]{0:T(1024)}, f32[1024]{0:T(1024)S(1)}, f32[768]{0:T(1024)}, f32[1024,768]{0,1:T(8,128)S(1)}) fusion(f32[1024,768]{0,1:T(8,128)} %copy-done.4, f32[1024]{0:T(1024)S(1)} %fusion.34, f32[1024]{0:T(1024)S(1)} %broadcast_multiply_fusion.1, f32[768]{0:T(1024)S(1)} %convert_element_type.193, ...), kind=kOutput, calls=%fused_computation.83 | convolution fusion | flops 4845204480 | bytes 22061056 | tf_op jit(solution)/shard_map/nf,df->nd/dot_general | solution.py:173
  381.7 2.9 fusion.47
  384.6 10.7 %fusion.37 = f32[768,3072]{1,0:T(8,128)} fusion(bf16[1024,3072]{1,0:T(8,128)(2,1)} %get-tuple-element.266, f32[1024,768]{0,1:T(8,128)} %copy-done.4, f32[768]{0:T(1024)S(1)} %copy-done.32, f32[768]{0:T(1024)S(1)} %convert_element_type.193, f32[1024]{0:T(1024)S(1)} %fusion.34, f32[1024]{0:T(1024)S(1)} %broadcast_multiply_fusion.1), kind=kOutput, calls=%fused_computation.137 | convolution fusion | flops 4835770368 | bytes 18888704 | tf_op jit(solution)/shard_map/nd,nf->df/dot_general | solution.py:172
  395.4 9.9 %fusion.48 = f32[3072,768]{1,0:T(8,128)} fusion(bf16[1024,3072]{1,0:T(8,128)(2,1)} %copy-done.39, bf16[1024,768]{0,1:T(8,128)(2,1)} %get-tuple-element.241), kind=kOutput, calls=%fused_computation.145 | convolution fusion | flops 4831838208 | bytes 17301504 | tf_op jit(solution)/shard_map/nf,nd->fd/dot_general | solution.py:168
  405.4 4.4 convolution_convert_fusion
  409.8 7.2 gather_fusion.7
  416.9 4.4 all-to-all-start.4
  421.4 59.2 %all-to-all-done.4 = bf16[8,128,768]{2,1,0:T(8,128)(2,1)} async-done(((bf16[8,128,768]{2,1,0:T(8,128)(2,1)}), bf16[8,128,768]{2,1,0:T(8,128)(2,1)}, u32[]{:S(2)}, u32[]{:S(2)}) %all-to-all-start.4) | async-done | bytes 1572896 | tf_op jit(solution)/shard_map/all_to_all | solution.py:183
  480.7 7.4 gather_fusion.8
  488.1 2.6 copy.105
  490.7 3.8 reshape.287
  494.5 30.4 %while.23 = (s32[]{:T(128)}, bf16[2,4,128,3,12,64]{2,1,0,5,4,3:T(4,128)(2,1)}, bf16[2,4,128,3,12,64]{2,5,4,1,3,0:T(8,128)(2,1)}, pred[2,4,128]{2,1,0:T(4,128)(4,...) while((s32[]{:T(128)}, ...), condition=%wide.region_19.20_spmd, body=%wide.region_17.19_spmd.sunk | while | flops 514713600 | bytes 86640328 | solution.py:187
  504.6 3.0 copy_dynamic-update-slice_fusion.5
  519.8 3.0 copy_dynamic-update-slice_fusion.5
  525.0 8.8 reshape.288
  533.7 6.7 copy.109
  540.4 13.1 %gather_fusion.9 = bf16[1024,2304]{1,0:T(8,128)(2,1)} fusion(bf16[1024,2304]{1,0:T(8,128)(2,1)} %copy.109, s32[1024]{0:T(1024)S(1)} %copy-done.18), kind=kCustom, calls=%fused_computation.9 | custom fusion | bytes 9441280 | tf_op jit(solution)/shard_map/gather | solution.py:190
  553.5 178.6 %all_to_all.66 = bf16[8,128,2304]{2,1,0:T(8,128)(2,1)} all-to-all(bf16[8,128,2304]{2,1,0:T(8,128)(2,1)} %bitcast.168), channel_id=1, replica_groups=mesh['grp'=4,'tok'=8] {'tok'}, dimensions={0} | all-to-all | bytes 9437184 | tf_op jit(solution)/shard_map/all_to_all | solution.py:189
  732.1 12.8 %gather_fusion.10 = bf16[1024,2304]{1,0:T(8,128)(2,1)} fusion(bf16[1024,2304]{1,0:T(8,128)(2,1)} %bitcast.166, s32[1024]{0:T(1024)S(1)} %copy-done.20), kind=kCustom, calls=%fused_computation.10 | custom fusion | bytes 9441280 | tf_op jit(solution)/shard_map/gather | solution.py:189
  744.9 9.6 %convolution_bitcast_fusion = f32[768,2304]{0,1:T(8,128)} fusion(bf16[1024,2304]{1,0:T(8,128)(2,1)} %gather_fusion.10, bf16[1024,768]{1,0:T(8,128)(2,1)} %param.21), kind=kOutput, calls=%fused_computation.72 | convolution fusion | flops 3623878656 | bytes 13369344 | tf_op jit(solution)/shard_map/nd,ne->de/dot_general | solution.py:192
  754.5 8.0 copy.120
  764.2 2.2 convert_element_type.224
  766.4 2.4 convert_element_type.229
  768.9 69.8 %reduce-scatter.13.cloned.1.call-done = f32[96,2304]{1,0:T(8,128)} async-done(((f32[768,2304]{1,0:T(8,128)}), f32[96,2304]{1,0:T(8,128)}) %reduce-scatter.13.cloned.1.call-update) | async-done | bytes 884752
  838.7 2.2 copy.121
  842.8 2.6 copy.111
  845.4 8.4 add_convert_fusion.2
  853.8 2.6 copy.112
  856.4 3.1 convert_reduce_fusion.1
  860.1 27.5 %all-reduce.9 = (bf16[768]{0:T(1024)(128)(2,1)}, bf16[768]{0:T(1024)(128)(2,1)}, bf16[768]{0:T(1024)(128)(2,1)}, bf16[768]{0:T(1024)(128)(2,1)}, bf16[768]{0:T(1...) all-reduce(f32[768]{0:T(1024)} %get-tuple-element.254, ...), channel_id=3, replica_groups=mesh['grp'=4,'tok'=8] {'tok'}, use_global_device_ids=true, to_apply=%region_23.24.clone | all-reduce | flops 9216 | bytes 55296
  897.3 11.2 %all-reduce.10 = (bf16[96]{0:T(256)(128)(2,1)}, bf16[96]{0:T(256)(128)(2,1)}, bf16[96]{0:T(256)(128)(2,1)}, bf16[96]{0:T(256)(128)(2,1)}, bf16[96]{0:T(256)(128)...) all-reduce(bf16[96]{0:T(256)(128)(2,1)S(1)} %dynamic-slice.35, ...), channel_id=1, replica_groups=mesh['grp'=4,'tok'=8] {'grp'}, use_global_device_ids=true, to_apply=%region_24.25 | all-reduce | flops 1152 | bytes 4608 | tf_op jit(solution)/shard_map/psum | solution.py:219
  918.4 2.2 copy.113
  922.2 2.2 convert_element_type.225
  (224 shorter events, 87.5 us)
Async XLA Ops:
  7.2 41.0 %copy-start = (bf16[768,2304]{1,0:T(8,128)(2,1)S(1)}, bf16[768,2304]{1,0:T(8,128)(2,1)}, u32[]{:S(2)}) copy-start(bf16[768,2304]{1,0:T(8,128)(2,1)} %param.22) | copy-start | bytes 10616836
  7.2 22.0 %copy-start.34 = (bf16[768]{0:T(1024)(128)(2,1)S(1)}, bf16[768]{0:T(1024)(128)(2,1)}, u32[]{:S(2)}) copy-start(bf16[768]{0:T(1024)(128)(2,1)} %param.24) | copy-start | bytes 4612
  12.4 21.8 %copy-start.27 = (s32[1024]{0:T(1024)}, s32[1024]{0:T(1024)S(1)}, u32[]{:S(2)}) copy-start(s32[1024]{0:T(1024)S(1)} %get-tuple-element.78) | copy-start | bytes 12292
  12.4 43.1 %copy-start.13 = (s32[1024]{0:T(1024)}, s32[1024]{0:T(1024)S(1)}, u32[]{:S(2)}) copy-start(s32[1024]{0:T(1024)S(1)} %fusion.31) | copy-start | bytes 12292
  22.8 20.2 %all-to-all-start.1 = ((s32[8,128,1]{1,2,0:T(1,128)}), s32[8,128,1]{1,2,0:T(1,128)S(1)}, u32[]{:S(2)}, u32[]{:S(2)}) async-start(s32[8,128,1]{1,2,0:T(1,128)} %bitcast.24), calls=%async_computation.1 | async-start | bytes 8192 | tf_op jit(solution)/shard_map/all_to_all | solution.py:126
  43.0 25.3 %all-to-all-start.2 = ((s32[8,128,1]{1,2,0:T(1,128)}), s32[8,128,1]{1,2,0:T(1,128)S(1)}, u32[]{:S(2)}, u32[]{:S(2)}) async-start(s32[8,128,1]{1,2,0:T(1,128)} %bitcast.30), calls=%async_computation.2 | async-start | bytes 8192 | tf_op jit(solution)/shard_map/all_to_all | solution.py:127
  68.3 110.9 %all-to-all-start = ((bf16[8,128,2304]{2,1,0:T(8,128)(2,1)}), bf16[8,128,2304]{2,1,0:T(8,128)(2,1)}, u32[]{:S(2)}, u32[]{:S(2)}) async-start(bf16[8,128,2304]{2,1,0:T(8,128)(2,1)} %bitcast.167), calls=%async_computation | async-start | bytes 9437184 | tf_op jit(solution)/shard_map/all_to_all | solution.py:125
  79.1 113.0 %copy-start.15 = (s32[1024]{0:T(1024)}, s32[1024]{0:T(1024)S(1)}, u32[]{:S(2)}) copy-start(s32[1024]{0:T(1024)S(1)} %fusion.32) | copy-start | bytes 12292
  84.2 150.4 %copy-start.17 = (s32[1024]{0:T(1024)}, s32[1024]{0:T(1024)S(1)}, u32[]{:S(2)}) copy-start(s32[1024]{0:T(1024)S(1)} %broadcast_clamp_fusion) | copy-start | bytes 12292
  207.5 5.8 copy-start.36
  217.3 1.4 copy-start.7
  217.3 2.3 copy-start.11
  219.6 1.1 copy-start.8
  219.6 1.1 copy-start.12
  224.8 1.4 copy-start.7
  224.8 2.3 copy-start.11
  227.1 1.1 copy-start.8
  227.1 1.1 copy-start.12
  241.8 42.1 %all-to-all-start.3 = ((bf16[8,128,768]{2,1,0:T(8,128)(2,1)}), bf16[8,128,768]{2,1,0:T(8,128)(2,1)}, u32[]{:S(2)}, u32[]{:S(2)}) async-start(bf16[8,128,768]{2,1,0:T(8,128)(2,1)} %bitcast.169), calls=%async_computation.3 | async-start | bytes 3145728 | tf_op jit(solution)/shard_map/all_to_all | solution.py:140
  246.1 5.3 copy-start.35
  246.1 5.8 copy-start.30
  246.1 7.1 copy-start.28
  246.1 516.5 %reduce-scatter.7.cloned.1.call-start = ((), (), s32[]{:S(2)}) async-start(), calls=%async_computation.10 | async-start | bytes 2654208 | tf_op jit(solution)/shard_map/reduce_scatter | solution.py:206
  262.2 28.9 %copy-start.19 = (s32[1024]{0:T(1024)}, s32[1024]{0:T(1024)S(1)}, u32[]{:S(2)}) copy-start(s32[1024]{0:T(1024)S(1)} %fusion.33) | copy-start | bytes 12292
  291.1 42.7 %slice-start.2 = ((s8[4718592]{0:T(1024)(128)(4,1)}), s8[4194304]{0:T(1024)(128)(4,1)S(1)}, s32[]{:S(2)}) async-start(s8[4718592]{0:T(1024)(128)(4,1)} %bitcast.179), calls=%async_computation.17 | async-start | bytes 8388608
  295.1 38.7 %copy-start.4 = (f32[1024,768]{0,1:T(8,128)}, f32[1024,768]{0,1:T(8,128)S(1)}, u32[]{:S(2)}) copy-start(f32[1024,768]{0,1:T(8,128)S(1)} %get-tuple-element.260) | copy-start | bytes 9437188
  295.1 0.7 copy-start.29
  295.1 0.8 copy-start.31
  295.9 37.9 %copy-start.33 = (f32[768]{0:T(1024)S(1)}, f32[768]{0:T(1024)}, u32[]{:S(2)}) copy-start(f32[768]{0:T(1024)} %convert_element_type.198) | copy-start | bytes 9220
  295.9 37.9 %slice-start.3 = ((s8[4718592]{0:T(1024)(128)(4,1)}), s8[524288]{0:T(1024)(128)(4,1)S(1)}, s32[]{:S(2)}) async-start(s8[4718592]{0:T(1024)(128)(4,1)} %bitcast.179), calls=%async_computation.18 | async-start | bytes 1048576
  333.7 6.1 copy-start.39
  333.8 6.0 copy-start.1
  341.5 2.3 copy-start.23
  365.0 12.1 %copy-start.5 = (f32[1024,768]{0,1:T(8,128)S(1)}, f32[1024,768]{0,1:T(8,128)}, u32[]{:S(2)}) copy-start(f32[1024,768]{0,1:T(8,128)} %copy-done.4) | copy-start | bytes 9437188
  378.0 1.6 copy-start.3
  378.0 3.7 copy-start.10
  378.0 2.5 copy-start.21
  380.5 1.1 copy-start.9
  381.7 3.0 copy-start.32
  384.6 379.7 %reduce-scatter.9.cloned.1.call-start = ((), (), s32[]{:S(2)}) async-start(), calls=%async_computation.11 | async-start | bytes 10616832 | tf_op jit(solution)/shard_map/reduce_scatter | solution.py:210
  395.4 371.0 %reduce-scatter.11.cloned.1.call-start = ((), (), s32[]{:S(2)}) async-start(), calls=%async_computation.12 | async-start | bytes 10616832 | tf_op jit(solution)/shard_map/reduce_scatter | solution.py:212
  405.4 4.4 copy-start.14
  416.9 63.7 %copy-start.16 = (s32[1024]{0:T(1024)S(1)}, s32[1024]{0:T(1024)}, u32[]{:S(2)}) copy-start(s32[1024]{0:T(1024)} %copy-done.15) | copy-start | bytes 12292
  416.9 63.7 %all-to-all-start.4 = ((bf16[8,128,768]{2,1,0:T(8,128)(2,1)}), bf16[8,128,768]{2,1,0:T(8,128)(2,1)}, u32[]{:S(2)}, u32[]{:S(2)}) async-start(bf16[8,128,768]{2,1,0:T(8,128)(2,1)} %bitcast.170), calls=%async_computation.4 | async-start | bytes 3145728 | tf_op jit(solution)/shard_map/all_to_all | solution.py:183
  421.4 417.3 %reduce-scatter.13.cloned.1.call-start = ((), (), s32[]{:S(2)}) async-start(), calls=%async_computation.13 | async-start | bytes 7962624
  488.1 6.4 copy-start.37
  497.5 1.4 copy-start.2
  502.0 2.3 slice-start
  503.1 1.4 slice-start.1
  507.6 2.2 copy-start.6
  512.7 1.5 copy-start.2
  517.2 2.2 slice-start
  518.4 1.4 slice-start.1
  522.8 2.2 copy-start.6
  533.7 6.7 copy-start.18
  553.5 178.6 %copy-start.20 = (s32[1024]{0:T(1024)S(1)}, s32[1024]{0:T(1024)}, u32[]{:S(2)}) copy-start(s32[1024]{0:T(1024)} %copy-done.19) | copy-start | bytes 12292
  762.5 155.9 %all-reduce.14.cloned.1.call-start = ((), (), s32[]{:S(2)}) async-start(), calls=%async_computation.14 | async-start | bytes 3833856 | tf_op jit(solution)/shard_map/psum | solution.py:218
  764.2 76.7 %copy-start.38 = (u32[32]{0:T(128)S(1)}, u32[32]{0:T(128)}, u32[]{:S(2)}) copy-start(u32[32]{0:T(128)} %constant.162) | copy-start | bytes 388
  768.9 76.5 %copy-start.22 = (f32[1024]{0:T(1024)S(1)}, f32[1024]{0:T(1024)}, u32[]{:S(2)}) copy-start(f32[1024]{0:T(1024)} %copy-done.21) | copy-start | bytes 12292
  856.4 3.7 copy-start.24
  856.4 3.7 copy-start.25
  856.4 3.7 copy-start.26
Sparse Core Ops, SparseCore 0:
  384.7 35.1 reduce-scatter.6
  422.2 119.3 reduce-scatter.8
  543.8 188.2 reduce-scatter.10
  762.6 75.9 reduce-scatter.12
  843.2 66.1 all-reduce.13
where the time goes:
time: 941 us; the launch traced here: 934 us
  waiting for transfers between devices  246 us (26%)
  blocking collectives  217 us (23%)
  local copies, waits for them, and re-layouts  216 us (23%)
  matrix products  145 us (15%)
  other arithmetic  67.4 us (7%)
  starting transfers between devices  26 us (3%)
  between operations  16 us (2%)
    all_to_all x1, blocking collectives, per_device(): lax.all_to_all(grad_qkv_c[local_pos], 'tok', split_axis=0, concat_axis=0,...  179 us
    all_to_all x1, waiting for transfers between devices, per_device(): lax.all_to_all(qkv_rows[sort_order], 'tok', split_axis=0, concat_axis=0,...  95 us
    unnamed x6, waiting for transfers between devices  69.9 us
    all_to_all x1, waiting for transfers between devices, per_device(): lax.all_to_all(grad_context[sort_order], 'tok', split_axis=0, concat_axis...  59.2 us
    dot_general x1, matrix products, per_device(): jnp.dot(normed1_low, w_up, preferred_element_type=jnp.float32)  37.8 us
    unnamed x89, local copies, waits for them, and re-layouts  36.3 us
    unnamed x1, blocking collectives  27.5 us
    all_to_all x1, waiting for transfers between devices, per_device(): lax.all_to_all(context_c[local_pos], 'tok', split_axis=0, concat_axis=0,...  21.7 us
  transfers between devices with their start and end apart: 10, of which 4 were waited for; matrix products, arithmetic and copies ran while one was open for 25% of the time, Pallas kernels for 0%

commit v1 on v0

v1 whole, which is shorter than its diff:
```python
import jax
import jax.numpy as jnp
from jax import lax
from jax.sharding import PartitionSpec as P

H = 12
CLU = 128

eps = 1e-12
masked_score = -1000000000.0


def norm_rows(values, scales, shifts):
    centre = values - jnp.mean(values, axis=-1, keepdims=True)
    spread = jnp.mean(centre * centre, axis=-1, keepdims=True)
    return centre * lax.rsqrt(spread + eps) * scales + shifts


def gelu_exact(values):
    return jax.nn.gelu(values, approximate=False)


def valid_tokens(lengths_row, offset, amount, cluster):
    padded = (lengths_row + cluster - 1) // cluster * cluster
    starts = jnp.cumsum(padded) - padded
    position = offset + jnp.arange(amount, dtype=jnp.int32)
    inside = (position[:, None] >= starts[None, :]) & (
        position[:, None] < (starts + lengths_row)[None, :]
    )
    return jnp.any(inside, axis=1)


def dot32(a, b):
    return jnp.dot(a, b, preferred_element_type=jnp.float32)


def move(one_hot, rows):
    return dot32(one_hot, rows).astype(jnp.bfloat16)


def move_back(one_hot, rows):
    picked = jnp.einsum("pi,pd->id", one_hot, rows, preferred_element_type=jnp.float32)
    return picked.astype(jnp.bfloat16)


def exchange(rows):
    return lax.all_to_all(rows, "tok", split_axis=0, concat_axis=0, tiled=True)


def per_device(
    tokens_in, w_qkv, b_query, b_value, w_out, b_out, norm1_gain, norm1_shift,
    w_up, b_up, w_down, b_down, norm2_gain, norm2_shift, out_grad, doc_lengths, cluster_slots,
):
    tok_dev, width = tokens_in.shape
    head_size = width // H
    clusters = tok_dev // CLU
    n_tok = lax.axis_size("tok")
    per_peer = tok_dev // n_tok
    my_index = lax.axis_index("tok")
    f32 = jnp.float32

    usable = valid_tokens(doc_lengths[0], my_index * tok_dev, tok_dev, CLU)
    dest = cluster_slots // tok_dev
    dest_hot = (dest[:, None] == jnp.arange(n_tok)[None, :]).astype(jnp.int32)
    rank = jnp.sum((jnp.cumsum(dest_hot, axis=0) - dest_hot) * dest_hot, axis=1)
    send_pos = dest * per_peer + rank
    send_hot = (jnp.arange(tok_dev)[:, None] == send_pos[None, :])
    note = (cluster_slots % tok_dev) * 2 + usable.astype(jnp.int32)
    sent_note = jnp.sum(jnp.where(send_hot, note[None, :], 0), axis=1)
    send_hot = send_hot.astype(jnp.bfloat16)
    got_note = exchange(sent_note)
    x_got = exchange(move(send_hot, tokens_in))
    g_got = exchange(move(send_hot, out_grad))
    place_hot = jnp.arange(tok_dev)[:, None] == (got_note // 2)[None, :]
    key_live = jnp.sum(jnp.where(place_hot, got_note[None, :] % 2, 0), axis=1) > 0
    place_hot = place_hot.astype(jnp.bfloat16)
    x = move(place_hot, x_got)

    bias_qkv = jnp.concatenate(
        [b_query.astype(f32), jnp.zeros((width,), f32), b_value.astype(f32)]
    )
    qkv = (dot32(x, w_qkv) + bias_qkv).astype(jnp.bfloat16)
    packed = qkv.reshape(clusters, CLU, 3, H, head_size)
    query, keys, value = packed[:, :, 0], packed[:, :, 1], packed[:, :, 2]
    scale = head_size ** (-0.5)
    scores = jnp.einsum("bqhd,bkhd->bhqk", query, keys, preferred_element_type=f32) * scale
    scores = jnp.where(key_live.reshape(clusters, 1, 1, CLU), scores, masked_score)
    expo = jnp.exp(scores - jnp.max(scores, axis=-1, keepdims=True))
    probs = expo / jnp.sum(expo, axis=-1, keepdims=True)
    weights = probs.astype(jnp.bfloat16)
    context = jnp.einsum("bhqk,bkhd->bqhd", weights, value, preferred_element_type=f32)
    context = context.astype(jnp.bfloat16).reshape(tok_dev, width)

    resid1 = x.astype(f32) + dot32(context, w_out) + b_out.astype(f32)
    normed1, norm1_back = jax.vjp(
        norm_rows, resid1, norm1_gain.astype(f32), norm1_shift.astype(f32)
    )
    normed1_low = normed1.astype(jnp.bfloat16)
    up_pre = dot32(normed1_low, w_up) + b_up.astype(f32)
    gelu_out, gelu_back = jax.vjp(gelu_exact, up_pre)
    gelu_low = gelu_out.astype(jnp.bfloat16)
    down_out = dot32(gelu_low, w_down) + b_down.astype(f32)
    normed2, norm2_back = jax.vjp(
        norm_rows, normed1 + down_out, norm2_gain.astype(f32), norm2_shift.astype(f32)
    )
    out_got = exchange(move_back(place_hot, normed2.astype(jnp.bfloat16)))
    block_out = move_back(send_hot, out_got)

    g = move(place_hot, g_got)
    grad_resid2, grad_gain2, grad_shift2 = norm2_back(g.astype(f32))
    grad_down = grad_resid2.astype(jnp.bfloat16)
    grad_b_down = jnp.sum(grad_down.astype(f32), axis=0)
    grad_w_down = jnp.einsum("nf,nd->fd", gelu_low, grad_down, preferred_element_type=f32)
    grad_gelu = jnp.einsum("nd,fd->nf", grad_down, w_down, preferred_element_type=f32)
    grad_up = gelu_back(grad_gelu)[0].astype(jnp.bfloat16)
    grad_b_up = jnp.sum(grad_up.astype(f32), axis=0)
    grad_w_up = jnp.einsum("nd,nf->df", normed1_low, grad_up, preferred_element_type=f32)
    grad_normed1 = grad_resid2 + jnp.einsum(
        "nf,df->nd", grad_up, w_up, preferred_element_type=f32
    )
    grad_resid1, grad_gain1, grad_shift1 = norm1_back(grad_normed1)
    grad_attn = grad_resid1.astype(jnp.bfloat16)
    grad_b_out = jnp.sum(grad_attn.astype(f32), axis=0)
    grad_w_out = jnp.einsum("nd,ne->de", context, grad_attn, preferred_element_type=f32)
    grad_context = jnp.einsum("ne,de->nd", grad_attn, w_out, preferred_element_type=f32)
    grad_context = grad_context.astype(jnp.bfloat16).reshape(clusters, CLU, H, head_size)

    grad_probs = jnp.einsum("bqhd,bkhd->bhqk", grad_context, value, preferred_element_type=f32)
    row_dot = jnp.sum(grad_probs * probs, axis=-1, keepdims=True)
    grad_scores = (probs * (grad_probs - row_dot)).astype(jnp.bfloat16)
    grad_q = jnp.einsum("bhqk,bkhd->bqhd", grad_scores, keys, preferred_element_type=f32) * scale
    grad_k = jnp.einsum("bhqk,bqhd->bkhd", grad_scores, query, preferred_element_type=f32) * scale
    grad_v = jnp.einsum("bhqk,bqhd->bkhd", weights, grad_context, preferred_element_type=f32)
    grad_qkv = jnp.stack([grad_q, grad_k, grad_v], axis=2).astype(jnp.bfloat16)
    grad_qkv = grad_qkv.reshape(tok_dev, 3 * width)
    grad_total = grad_resid1 + jnp.einsum(
        "ne,de->nd", grad_qkv, w_qkv, preferred_element_type=f32
    )
    back_got = exchange(move_back(place_hot, grad_total.astype(jnp.bfloat16)))
    grad_tokens = move_back(send_hot, back_got)
    grad_w_qkv = jnp.einsum("nd,ne->de", x, grad_qkv, preferred_element_type=f32)
    grad_qkv_sum = jnp.sum(grad_qkv.astype(f32), axis=0)

    low = jnp.bfloat16
    wide = jnp.concatenate(
        [
            grad_w_qkv.astype(low), grad_w_out.astype(low), grad_w_up.astype(low),
            grad_w_down.astype(low).reshape(width, -1),
        ],
        axis=1,
    )
    narrow = jnp.concatenate(
        [
            member.reshape(n_tok, -1)
            for member in (
                grad_qkv_sum[:width], grad_qkv_sum[2 * width :], grad_b_out, grad_gain1,
                grad_shift1, grad_b_down, grad_gain2, grad_shift2, grad_b_up,
            )
        ],
        axis=1,
    )
    share = lax.psum_scatter(wide, "tok", scatter_dimension=0, tiled=True)
    share = lax.psum(share, "grp").astype(f32)
    narrow = lax.psum(narrow, ("grp", "tok"))
    mine = lax.dynamic_index_in_dim(narrow, my_index, 0, keepdims=False)
    step = width // n_tok
    parts = [mine[i * step : (i + 1) * step] for i in range(8)] + [mine[8 * step :]]
    ffw = w_up.shape[1]
    return (
        block_out,
        grad_tokens,
        share[:, : 3 * width],
        parts[0],
        parts[1],
        share[:, 3 * width : 4 * width],
        parts[2],
        parts[3],
        parts[4],
        share[:, 4 * width : 4 * width + ffw],
        parts[8],
        share[:, 4 * width + ffw :].reshape(ffw // n_tok, width),
        parts[5],
        parts[6],
        parts[7],
    )


def solution(mesh):
    rows = P(("grp", "tok"), None)
    in_specs = (rows,) + (P(),) * 13 + (rows, P("grp", None), P(("grp", "tok")))
    shares = (
        P("tok", None), P("tok"), P("tok"), P("tok", None), P("tok"), P("tok"), P("tok"),
        P("tok", None), P("tok"), P("tok", None), P("tok"), P("tok"), P("tok"),
    )
    return jax.shard_map(
        per_device, mesh=mesh, in_specs=in_specs, out_specs=(rows, rows) + shares, check_vma=False
    )
```

time: 941 us -> 588 us (0.62)
  blocking collectives: 217 us -> 55.8 us
  local copies, waits for them, and re-layouts: 216 us -> 72.4 us
  waiting for transfers between devices: 246 us -> 199 us
  matrix products: 145 us -> 167 us
  other arithmetic: 67.4 us -> 46.7 us
    all_to_all x1 -> x0, blocking collectives: 179 us -> none  [per_device(): lax.all_to_all(grad_qkv_c[local_pos], 'tok', split_axis=0, concat_axis=0,...]
    reduce_scatter x3 -> x1, waiting for transfers between devices: 0.02 us -> 113 us  [per_device(): share = lax.psum_scatter(wide, 'tok', scatter_dimension=0, tiled=True)]
    gather x13 -> x0, local copies, waits for them, and re-layouts: 111 us -> none  [the longest x2 19.4 us: per_device(): cluster_qkv = got_rows[placing]]
    all_to_all x5, waiting for transfers between devices: 176 us -> 83.5 us  [exchange(): return lax.all_to_all(rows, 'tok', split_axis=0, concat_axis=0, tiled=True)]
    unnamed x6 -> x2, waiting for transfers between devices: 69.9 us -> 0.03 us
    psum x1, blocking collectives: 11.2 us -> 55.8 us  [per_device(): narrow = lax.psum(narrow, ('grp', 'tok'))]
    unnamed x1 -> x0, blocking collectives: 27.5 us -> none
    dot_general x26 -> x25, matrix products: 145 us -> 167 us  [the longest x8 70 us: dot32(): return jnp.dot(a, b, preferred_element_type=jnp.float32)]
  transfers between devices with their start and end apart: 10 -> 7, of which waited for: 4 -> 5; matrix products, arithmetic and copies ran while one was open for 25% -> 22% of each run, Pallas kernels for 0% -> 0%
where the time goes in v1:
time: 588 us; the launch traced here: 581 us
  waiting for transfers between devices  199 us (34%)
  matrix products  167 us (28%)
  local copies, waits for them, and re-layouts  72.4 us (12%)
  blocking collectives  55.8 us (9%)
  other arithmetic  46.7 us (8%)
  starting transfers between devices  24.7 us (4%)
  between operations  15.3 us (3%)
    reduce_scatter x1, waiting for transfers between devices, per_device(): share = lax.psum_scatter(wide, 'tok', scatter_dimension=0, tiled=True)  113 us
    all_to_all x5, waiting for transfers between devices, exchange(): return lax.all_to_all(rows, 'tok', split_axis=0, concat_axis=0, tiled=True)  83.5 us
    dot_general x8, matrix products, dot32(): return jnp.dot(a, b, preferred_element_type=jnp.float32)  70 us
    psum x1, blocking collectives, per_device(): narrow = lax.psum(narrow, ('grp', 'tok'))  55.8 us
    dot_general x4, matrix products, move_back(): jnp.einsum('pi,pd->id', one_hot, rows, preferred_element_type=jnp.float32)  25 us
    all_to_all x5, starting transfers between devices, exchange(): return lax.all_to_all(rows, 'tok', split_axis=0, concat_axis=0, tiled=True)  24.4 us
    dot_general x1, matrix products, per_device(): jnp.einsum('nd,fd->nf', grad_down, w_down, preferred_element_type=f32)  17.3 us
    unnamed x118, local copies, waits for them, and re-layouts  16.6 us
  transfers between devices with their start and end apart: 7, of which 5 were waited for; matrix products, arithmetic and copies ran while one was open for 22% of the time, Pallas kernels for 0%

profile of v1, /device:TPU:0, one launch (start us, length us, event | category | flops | bytes accessed | tf_op | source)
XLA Modules:
  0.0 581.2 jit_solution(15777151747984657836)
XLA Ops:
  10.3 5.1 reduce-window.9
  18.6 6.3 %all-to-all-start = ((s32[8,128,1]{1,2,0:T(1,128)}), s32[8,128,1]{1,2,0:T(1,128)S(1)}, u32[]{:S(2)}, u32[]{:S(2)}) async-start(s32[8,128,1]{1,2,0:T(1,128)} %bitcast.5), calls=%async_computation | async-start | bytes 8192 | tf_op jit(solution)/shard_map/all_to_all | solution.py:47
  24.9 4.5 fusion.48
  30.4 4.3 all-to-all-start.1
  38.0 1.3 convert_element_type.160
  41.8 4.5 fusion.50
  47.5 25.0 %all-to-all-done.1 = bf16[8,128,768]{2,1,0:T(8,128)(2,1)} async-done(((bf16[8,128,768]{2,1,0:T(8,128)(2,1)}), bf16[8,128,768]{2,1,0:T(8,128)(2,1)}, u32[]{:S(2)}, u32[]{:S(2)}) %all-to-all-start.1) | async-done | bytes 1572896 | tf_op jit(solution)/shard_map/all_to_all | solution.py:47
  72.6 4.3 all-to-all-start.3
  77.2 3.3 fusion.52
  81.6 5.5 add_convert_fusion.1
  87.2 6.7 %copy.79 = bf16[1024,2304]{0,1:T(8,128)(2,1)} copy(bf16[1024,2304]{1,0:T(8,128)(2,1)} %add_convert_fusion.1) | data formatting | bytes 9437184 | tf_op jit(solution)/shard_map/convert_element_type | solution.py:82
  93.9 3.6 copy.107
  100.5 2.7 fusion.101
  104.2 1.7 copy-done.9
  107.6 1.6 fusion.102
  110.0 1.9 copy-done.32
  111.9 37.4 %multiply_convert_fusion = (bf16[1024,3072]{1,0:T(8,128)(2,1)S(1)}, f32[1024,3072]{1,0:T(8,128)}, f32[1024,3072]{1,0:T(8,128)}) fusion(f32[3072]{0:T(1024)S(1)} %copy-done.32, bf16[768,3072]{1,0:T(8,128)(2,1)S(1)} %bitcast.169, f32[1024,768]{0,1:T(8,128)S(1)} %get-tuple-element.59, f32[768]{0:T(1024)S(1)} %copy-done.34, f32[768]{0:T(1024)S(1)} %convert_element_type.157, ...), kind=kOutput, calls=%fused_computation.6 | convolution fusion | flops 5043388416 | bytes 39348224 | tf_op jit(solution)/shard_map/dot_general | solution.py:34
  149.4 7.5 %fusion.103 = (f32[1024]{0:T(1024)S(1)}, f32[1024,768]{0,1:T(8,128)}) fusion(f32[768]{0:T(1024)S(1)} %copy-done.36, bf16[1024,3072]{1,0:T(8,128)(2,1)S(1)} %get-tuple-element.31, bf16[3072,768]{1,0:T(8,128)(2,1)S(1)} %bitcast.167, f32[768]{0:T(1024)S(1)} %copy-done.34, f32[768]{0:T(1024)S(1)} %convert_element_type.157, f32[1024]{0:T(1024)S(1)} %fusion.85, ...), kind=kOutput, calls=%fused_computation.186 | convolution fusion | flops 4837342208 | bytes 17323008 | tf_op jit(solution)/shard_map/dot_general | solution.py:34
  156.9 5.6 fusion.22
  162.6 2.2 fusion.23
  164.8 1.9 convert_reduce_fusion.3
  167.6 7.1 %convolution_convert_fusion = bf16[3072,768]{1,0:T(8,128)(2,1)} fusion(bf16[1024,3072]{1,0:T(8,128)(2,1)S(1)} %copy-done.47, bf16[1024,768]{0,1:T(8,128)(2,1)S(1)} %get-tuple-element.24), kind=kOutput, calls=%fused_computation.27 | convolution fusion | flops 4834197504 | bytes 12582912 | tf_op jit(solution)/shard_map/nf,nd->fd/dot_general | solution.py:113
  174.7 17.3 %convert_reduce_fusion = (f32[3072]{0:T(1024)}, bf16[1024,3072]{1,0:T(8,128)(2,1)}) fusion(f32[1024,3072]{1,0:T(8,128)} %get-tuple-element.32, bf16[1024,768]{0,1:T(8,128)(2,1)} %copy-done.18, bf16[3072,768]{1,0:T(8,128)(2,1)} %param.27, f32[1024,3072]{1,0:T(8,128)} %get-tuple-element.60, f32[3072]{0:T(1024)} %convert_element_type.160), kind=kOutput, calls=%fused_computation.4 | convolution fusion | flops 4885312512 | bytes 37773312 | tf_op jit(solution)/shard_map/nd,fd->nf/dot_general | solution.py:114
  192.1 10.6 %convolution_convert_fusion.1 = bf16[768,3072]{1,0:T(8,128)(2,1)} fusion(bf16[1024,3072]{1,0:T(8,128)(2,1)} %get-tuple-element.68, f32[1024,768]{0,1:T(8,128)} %copy-done.6, f32[768]{0:T(1024)S(1)} %copy-done.35, f32[768]{0:T(1024)S(1)} %copy-done.24, f32[1024]{0:T(1024)S(1)} %copy-done.26, f32[1024]{0:T(1024)S(1)} %broadcast_multiply_fusion.1), kind=kOutput, calls=%fused_computation.28 | convolution fusion | flops 4838129664 | bytes 14170112 | tf_op jit(solution)/shard_map/nd,nf->df/dot_general | solution.py:117
  202.7 10.1 %multiply_reduce_fusion.1 = (f32[768]{0:T(1024)}, f32[1024]{0:T(1024)S(1)}, f32[768]{0:T(1024)}, f32[1024,768]{0,1:T(8,128)S(1)}) fusion(f32[1024,768]{0,1:T(8,128)S(1)} %copy-done.7, f32[1024]{0:T(1024)S(1)} %copy-done.26, f32[1024]{0:T(1024)S(1)} %broadcast_multiply_fusion.1, f32[768]{0:T(1024)S(1)} %copy-done.24, bf16[1024,3072]{1,0:T(8,128)(2,1)S(1)} %copy-done.45, ...), kind=kOutput, calls=%fused_computation.57 | convolution fusion | flops 4845204480 | bytes 22061056 | tf_op jit(solution)/shard_map/nf,df->nd/dot_general | solution.py:118
  214.6 1.6 copy-done.17
  216.2 2.4 fusion.63
  218.6 2.6 convolution_convert_fusion.3
  221.2 2.8 copy.87
  224.0 2.0 copy.109
  226.0 7.1 %multiply_reduce_fusion = (f32[8,12,128]{2,1,0:T(8,128)S(1)}, f32[8,12,128,128]{2,3,1,0:T(8,128)}) fusion(f32[8,12,128,128]{2,3,1,0:T(8,128)} %copy-done.9, f32[8,12,128]{2,1,0:T(8,128)S(1)} %copy-done.20, bf16[8,128,1,12,64]{1,0,4,3,2:T(8,128)(2,1)S(1)} %copy-done.15, bf16[8,128,12,64]{1,0,3,2:T(8,128)(2,1)S(1)} %bitcast.160), kind=kOutput, calls=%fused_computation.24 | convolution fusion | flops 206032896 | bytes 15826944 | tf_op jit(solution)/shard_map/bqhd,bkhd->bhqk/dot_general | solution.py:128
  233.1 5.0 multiply_convert_fusion.1
  238.1 2.1 multiply_bitcast_fusion.1
  240.2 3.4 multiply_bitcast_fusion
  243.6 3.4 convolution_bitcast_fusion
  247.1 8.5 %reshape.307 = bf16[768,3072]{1,0:T(8,128)(2,1)} reshape(bf16[3072,768]{1,0:T(8,128)(2,1)} %convolution_convert_fusion) | data formatting | bytes 9437184 | tf_op jit(solution)/shard_map/reshape | solution.py:148
  255.5 2.4 copy.95
  257.9 4.0 convert_reduce_fusion.1
  261.9 9.2 %copy.93 = bf16[8,128,3,12,64]{1,0,4,3,2:T(8,128)(2,1)S(1)} copy(bf16[8,128,3,12,64]{1,4,3,0,2:T(8,128)(2,1)S(1)} %get-tuple-element.28) | data formatting | bytes 9437184 | tf_op jit(solution)/shard_map/convert_element_type | solution.py:134
  271.2 4.1 convolution_convert_fusion.2
  276.7 9.5 %pad_maximum_fusion = bf16[768,9216]{1,0:T(8,128)(2,1)} fusion(bf16[768,3072]{1,0:T(8,128)(2,1)S(1)} %bitcast.145, bf16[768,3072]{1,0:T(8,128)(2,1)S(1)} %bitcast.152, bf16[768,768]{1,0:T(8,128)(2,1)S(1)} %copy-done.12, bf16[768,2304]{1,0:T(8,128)(2,1)S(1)} %convolution_convert_fusion.2), kind=kLoop, calls=%fused_computation.2 | loop fusion | flops 56623104 | bytes 28311552 | tf_op jit(solution)/shard_map/concatenate | solution.py:145
  286.2 10.0 %fusion.45 = bf16[1024,768]{1,0:T(8,128)(2,1)} fusion(s32[1024]{0:T(1024)} %copy-done.29, f32[1024,768]{0,1:T(8,128)} %copy-done.8, bf16[768,2304]{1,0:T(8,128)(2,1)S(1)} %copy-done, bf16[288,8,8,128]{3,2,1,0:T(8,128)(2,1)} %bitcast.154, f32[1024]{0:T(1024)S(1)} %negate_multiply_fusion.1), kind=kOutput, calls=%fused_computation.89 | convolution fusion | flops 5239734272 | bytes 12984320 | tf_op jit(solution)/shard_map/pi,pd->id/dot_general | solution.py:42
  296.2 5.1 all-to-all-start.4
  302.0 5.2 fusion.42
  307.2 57.5 %all-to-all-done.4 = bf16[8,128,768]{2,1,0:T(8,128)(2,1)} async-done(((bf16[8,128,768]{2,1,0:T(8,128)(2,1)}), bf16[8,128,768]{2,1,0:T(8,128)(2,1)}, u32[]{:S(2)}, u32[]{:S(2)}) %all-to-all-start.4) | async-done | bytes 1572896 | tf_op jit(solution)/shard_map/all_to_all | solution.py:47
  364.7 4.3 all-to-all-start.2
  369.1 113.2 %reduce-scatter.2.cloned.1.call-done = bf16[96,9216]{1,0:T(8,128)(2,1)} async-done(((bf16[768,9216]{1,0:T(8,128)(2,1)}), bf16[96,9216]{1,0:T(8,128)(2,1)}) %reduce-scatter.2.cloned.1.call-update) | async-done | bytes 1769488 | tf_op jit(solution)/shard_map/reduce_scatter | solution.py:162
  483.8 1.3 reshape.308
  485.2 1.4 reshape.309
  486.5 1.3 reshape.310
  488.6 1.3 reshape.311
  489.9 1.3 reshape.312
  491.3 1.3 reshape.313
  492.6 1.4 concatenate.11
  494.0 55.8 %psum.15 = f32[8,1152]{1,0:T(8,128)} all-reduce(f32[8,1152]{1,0:T(8,128)} %concatenate.11), channel_id=1, replica_groups=mesh['grp'=4,'tok'=8] {'grp','tok'}, use_global_device_ids=true, to_apply=%region_28.29 | all-reduce | flops 9216 | bytes 73728 | tf_op jit(solution)/shard_map/psum | solution.py:164
  549.9 1.4 dynamic-slice_reduce_fusion
  551.3 1.4 dynamic-slice_bitcast_fusion
  552.7 5.0 fusion.51
  557.7 4.8 fusion.49
  562.5 2.3 all-reduce.2.cloned.1.call-done
  564.8 2.9 fusion.99
  567.7 2.6 reshape.315
  570.3 2.0 slice.132
  572.2 1.6 slice.135
  (169 shorter events, 29.1 us)
Async XLA Ops:
  7.2 74.5 %copy-start = (bf16[768,2304]{1,0:T(8,128)(2,1)S(1)}, bf16[768,2304]{1,0:T(8,128)(2,1)}, u32[]{:S(2)}) copy-start(bf16[768,2304]{1,0:T(8,128)(2,1)} %param.18) | copy-start | bytes 10616836
  17.5 24.4 %copy-start.27 = (s32[1024]{0:T(1024)}, s32[1024]{0:T(1024)S(1)}, u32[]{:S(2)}) copy-start(s32[1024]{0:T(1024)S(1)} %multiply_add_fusion.3) | copy-start | bytes 12292
  18.6 11.8 %all-to-all-start = ((s32[8,128,1]{1,2,0:T(1,128)}), s32[8,128,1]{1,2,0:T(1,128)S(1)}, u32[]{:S(2)}, u32[]{:S(2)}) async-start(s32[8,128,1]{1,2,0:T(1,128)} %bitcast.5), calls=%async_computation | async-start | bytes 8192 | tf_op jit(solution)/shard_map/all_to_all | solution.py:47
  29.4 5.3 copy-start.38
  29.4 5.3 copy-start.39
  30.4 16.0 %copy-start.31 = (s32[8,128,1]{1,2,0:T(1,128)}, s32[8,128,1]{1,2,0:T(1,128)S(1)}, u32[]{:S(2)}) copy-start(s32[8,128,1]{1,2,0:T(1,128)S(1)} %all-to-all-done) | copy-start | bytes 12292
  30.4 42.2 %all-to-all-start.1 = ((bf16[8,128,768]{2,1,0:T(8,128)(2,1)}), bf16[8,128,768]{2,1,0:T(8,128)(2,1)}, u32[]{:S(2)}, u32[]{:S(2)}) async-start(bf16[8,128,768]{2,1,0:T(8,128)(2,1)} %bitcast.159), calls=%async_computation.1 | async-start | bytes 3145728 | tf_op jit(solution)/shard_map/all_to_all | solution.py:47
  36.7 112.6 %copy-start.23 = (f32[768]{0:T(1024)}, f32[768]{0:T(1024)S(1)}, u32[]{:S(2)}) copy-start(f32[768]{0:T(1024)S(1)} %convert_element_type.157) | copy-start | bytes 9220
  47.0 33.4 %copy-start.29 = (s32[1024]{0:T(1024)}, s32[1024]{0:T(1024)S(1)}, u32[]{:S(2)}) copy-start(s32[1024]{0:T(1024)S(1)} %get-tuple-element.51) | copy-start | bytes 12292
  72.6 84.3 %all-to-all-start.3 = ((bf16[8,128,768]{2,1,0:T(8,128)(2,1)}), bf16[8,128,768]{2,1,0:T(8,128)(2,1)}, u32[]{:S(2)}, u32[]{:S(2)}) async-start(bf16[8,128,768]{2,1,0:T(8,128)(2,1)} %bitcast.158), calls=%async_computation.3 | async-start | bytes 3145728 | tf_op jit(solution)/shard_map/all_to_all | solution.py:47
  76.9 405.4 %reduce-scatter.2.cloned.1.call-start = ((), (), s32[]{:S(2)}) async-start(), calls=%async_computation.6 | async-start | bytes 15925248 | tf_op jit(solution)/shard_map/reduce_scatter | solution.py:162
  77.2 4.5 copy-start.33
  97.8 1.1 copy-start.1
  97.8 1.6 copy-start.3
  97.8 5.3 copy-start.14
  103.2 2.7 copy-start.9
  103.2 2.7 copy-start.19
  105.9 1.3 copy-start.37
  105.9 1.3 copy-start.40
  105.9 1.8 copy-start.43
  107.1 2.2 copy-start.16
  107.1 2.9 slice-start.8
  107.6 2.4 slice-start.9
  107.6 41.7 %slice-start.6 = ((s8[4718592]{0:T(1024)(128)(4,1)}), s8[4194304]{0:T(1024)(128)(4,1)S(1)}, s32[]{:S(2)}) async-start(s8[4718592]{0:T(1024)(128)(4,1)} %bitcast.166), calls=%async_computation.14 | async-start | bytes 8388608
  109.3 40.0 %copy-start.6 = (f32[1024,768]{0,1:T(8,128)}, f32[1024,768]{0,1:T(8,128)S(1)}, u32[]{:S(2)}) copy-start(f32[1024,768]{0,1:T(8,128)S(1)} %get-tuple-element.59) | copy-start | bytes 9437188
  109.3 2.6 copy-start.32
  109.3 2.6 copy-start.34
  109.7 39.6 %copy-start.21 = (f32[1024]{0:T(1024)}, f32[1024]{0:T(1024)S(1)}, u32[]{:S(2)}) copy-start(f32[1024]{0:T(1024)S(1)} %multiply_reduce_fusion.4) | copy-start | bytes 12292
  111.9 37.4 %copy-start.25 = (f32[1024]{0:T(1024)}, f32[1024]{0:T(1024)S(1)}, u32[]{:S(2)}) copy-start(f32[1024]{0:T(1024)S(1)} %fusion.85) | copy-start | bytes 12292
  111.9 37.5 %copy-start.36 = (f32[768]{0:T(1024)S(1)}, f32[768]{0:T(1024)}, u32[]{:S(2)}) copy-start(f32[768]{0:T(1024)} %convert_element_type.162) | copy-start | bytes 9220
  111.9 37.5 %slice-start.7 = ((s8[4718592]{0:T(1024)(128)(4,1)}), s8[524288]{0:T(1024)(128)(4,1)S(1)}, s32[]{:S(2)}) async-start(s8[4718592]{0:T(1024)(128)(4,1)} %bitcast.166), calls=%async_computation.15 | async-start | bytes 1048576
  149.3 7.6 %copy-start.46 = (bf16[1024,3072]{1,0:T(8,128)(2,1)}, bf16[1024,3072]{1,0:T(8,128)(2,1)S(1)}, u32[]{:S(2)}) copy-start(bf16[1024,3072]{1,0:T(8,128)(2,1)S(1)} %get-tuple-element.31) | copy-start | bytes 18874372
  156.9 5.7 copy-start.5
  162.5 4.1 copy-start.10
  164.8 2.8 copy-start.47
  166.7 8.0 %copy-start.18 = (bf16[1024,768]{0,1:T(8,128)(2,1)}, bf16[1024,768]{0,1:T(8,128)(2,1)S(1)}, u32[]{:S(2)}) copy-start(bf16[1024,768]{0,1:T(8,128)(2,1)S(1)} %get-tuple-element.24) | copy-start | bytes 4718596
  174.7 17.3 %copy-start.24 = (f32[768]{0:T(1024)S(1)}, f32[768]{0:T(1024)}, u32[]{:S(2)}) copy-start(f32[768]{0:T(1024)} %copy-done.23) | copy-start | bytes 9220
  174.7 17.3 %copy-start.26 = (f32[1024]{0:T(1024)S(1)}, f32[1024]{0:T(1024)}, u32[]{:S(2)}) copy-start(f32[1024]{0:T(1024)} %copy-done.25) | copy-start | bytes 12292
  174.7 17.3 %copy-start.35 = (f32[768]{0:T(1024)S(1)}, f32[768]{0:T(1024)}, u32[]{:S(2)}) copy-start(f32[768]{0:T(1024)} %convert_element_type.158) | copy-start | bytes 9220
  192.1 10.7 %copy-start.7 = (f32[1024,768]{0,1:T(8,128)S(1)}, f32[1024,768]{0,1:T(8,128)}, u32[]{:S(2)}) copy-start(f32[1024,768]{0,1:T(8,128)} %copy-done.6) | copy-start | bytes 9437188
  192.1 10.6 %copy-start.11 = (bf16[1024,768]{0,1:T(8,128)(2,1)S(1)}, bf16[1024,768]{0,1:T(8,128)(2,1)}, u32[]{:S(2)}) copy-start(bf16[1024,768]{0,1:T(8,128)(2,1)} %copy-done.10) | copy-start | bytes 4718596
  192.1 10.6 %copy-start.45 = (bf16[1024,3072]{1,0:T(8,128)(2,1)S(1)}, bf16[1024,3072]{1,0:T(8,128)(2,1)}, u32[]{:S(2)}) copy-start(bf16[1024,3072]{1,0:T(8,128)(2,1)} %get-tuple-element.68) | copy-start | bytes 18874372
  202.7 10.1 %copy-start.22 = (f32[1024]{0:T(1024)S(1)}, f32[1024]{0:T(1024)}, u32[]{:S(2)}) copy-start(f32[1024]{0:T(1024)} %copy-done.21) | copy-start | bytes 12292
  213.6 5.0 copy-start.8
  213.6 2.5 copy-start.17
  216.2 2.4 copy-start.41
  224.0 2.0 copy-start.15
  224.0 2.0 copy-start.20
  226.0 7.1 %slice-start.2 = ((s8[6291456]{0:T(1024)(128)(4,1)}), s8[4194304]{0:T(1024)(128)(4,1)S(1)}, s32[]{:S(2)}) async-start(s8[6291456]{0:T(1024)(128)(4,1)} %bitcast.149), calls=%async_computation.10 | async-start | bytes 8388608
  226.0 7.1 %slice-start.3 = ((s8[6291456]{0:T(1024)(128)(4,1)}), s8[2097152]{0:T(1024)(128)(4,1)S(1)}, s32[]{:S(2)}) async-start(s8[6291456]{0:T(1024)(128)(4,1)} %bitcast.149), calls=%async_computation.11 | async-start | bytes 4194304
  233.1 5.0 copy-start.4
  238.1 2.1 copy-start.2
  261.9 9.3 %copy-start.44 = (bf16[1024,768]{0,1:T(8,128)(2,1)S(1)}, bf16[1024,768]{0,1:T(8,128)(2,1)}, u32[]{:S(2)}) copy-start(bf16[1024,768]{0,1:T(8,128)(2,1)} %copy-done.42) | copy-start | bytes 4718596
  261.9 13.4 %slice-start = ((s8[4718592]{0:T(1024)(128)(4,1)}), s8[524288]{0:T(1024)(128)(4,1)S(1)}, s32[]{:S(2)}) async-start(s8[4718592]{0:T(1024)(128)(4,1)} %bitcast.144), calls=%async_computation.8 | async-start | bytes 1048576
  261.9 13.4 %slice-start.4 = ((s8[4718592]{0:T(1024)(128)(4,1)}), s8[524288]{0:T(1024)(128)(4,1)S(1)}, s32[]{:S(2)}) async-start(s8[4718592]{0:T(1024)(128)(4,1)} %bitcast.151), calls=%async_computation.12 | async-start | bytes 1048576
  271.2 4.2 copy-start.13
  271.2 4.2 slice-start.1
  271.2 4.2 copy-start.12
  271.2 5.5 slice-start.5
  296.2 5.8 copy-start.30
  296.2 68.5 %all-to-all-start.4 = ((bf16[8,128,768]{2,1,0:T(8,128)(2,1)}), bf16[8,128,768]{2,1,0:T(8,128)(2,1)}, u32[]{:S(2)}, u32[]{:S(2)}) async-start(bf16[8,128,768]{2,1,0:T(8,128)(2,1)} %bitcast.162), calls=%async_computation.4 | async-start | bytes 3145728 | tf_op jit(solution)/shard_map/all_to_all | solution.py:47
  364.7 192.9 %all-to-all-start.2 = ((bf16[8,128,768]{2,1,0:T(8,128)(2,1)}), bf16[8,128,768]{2,1,0:T(8,128)(2,1)}, u32[]{:S(2)}, u32[]{:S(2)}) async-start(bf16[8,128,768]{2,1,0:T(8,128)(2,1)} %bitcast.155), calls=%async_computation.2 | async-start | bytes 3145728 | tf_op jit(solution)/shard_map/all_to_all | solution.py:47
  369.1 195.7 %all-reduce.2.cloned.1.call-start = ((), (), s32[]{:S(2)}) async-start(), calls=%async_computation.7 | async-start | bytes 3538944 | tf_op jit(solution)/shard_map/psum | solution.py:163
  552.7 5.0 copy-start.28
  (1 other events, 1.1 us)
Sparse Core Ops, SparseCore 0:
  286.3 195.9 reduce-scatter.1
  485.5 79.2 all-reduce.1

commit v2 on v1

--- a/solution.py
+++ b/solution.py
@@ -1,6 +1,10 @@
+import functools
+
 import jax
 import jax.numpy as jnp
 from jax import lax
+from jax.experimental import pallas as pl
+from jax.experimental.pallas import tpu as pltpu
 from jax.sharding import PartitionSpec as P
 
 H = 12
@@ -9,11 +13,341 @@
 eps = 1e-12
 masked_score = -1000000000.0
 
-
-def norm_rows(values, scales, shifts):
+MESH = pl.DeviceIdType.MESH
+f32 = jnp.float32
+bf16 = jnp.bfloat16
+BLK = 256
+
+
+def dot32(a, b):
+    return jnp.dot(a, b, preferred_element_type=jnp.float32)
+
+
+def dot_rows(a, b):
+    return lax.dot_general(a, b, (((1,), (1,)), ((), ())), preferred_element_type=jnp.float32)
+
+
+def dot_cols(a, b):
+    return lax.dot_general(a, b, (((0,), (0,)), ((), ())), preferred_element_type=jnp.float32)
+
+
+def peer_order(n_tok):
+    return sorted(range(1, n_tok), key=lambda k: -k)
+
+
+def row_of(ref):
+    return ref[...].astype(f32)[None, :]
+
+
+def norm_parts(values):
     centre = values - jnp.mean(values, axis=-1, keepdims=True)
     spread = jnp.mean(centre * centre, axis=-1, keepdims=True)
-    return centre * lax.rsqrt(spread + eps) * scales + shifts
+    rstd = lax.rsqrt(spread + eps)
+    return centre * rstd, rstd
+
+
+def lane_halves(width):
+    lane = lax.broadcasted_iota(jnp.int32, (1, width), 1)
+    low = (lane < width // 2).astype(f32)
+    return low.astype(bf16), (1.0 - low).astype(bf16)
+
+
+def stack_heads(pair, halves):
+    return jnp.concatenate([pair * halves[0], pair * halves[1]], axis=0)
+
+
+def side_by_side(stacked):
+    half = stacked.shape[0] // 2
+    return jnp.concatenate([stacked[:half], stacked[half:]], axis=1)
+
+
+def column_of(row):
+    amount = row.shape[1]
+    return jnp.concatenate(
+        [
+            jnp.broadcast_to(row[:, at : at + 128], (128, 128)).T
+            for at in range(0, amount, 128)
+        ],
+        axis=0,
+    )
+
+
+def hot_from_column(column, amount):
+    lane = lax.broadcasted_iota(jnp.int32, column.shape, 1).astype(f32)
+    return jnp.concatenate(
+        [(lane + float(at) == column).astype(f32).astype(bf16) for at in range(0, amount, 128)],
+        axis=1,
+    )
+
+
+def forward_kernel(
+    n_tok, per,
+    slots_ref, docs_ref, tok_ref, og_ref, wq_ref, bq_ref, bv_ref, wo_ref, bo_ref, g1_ref, s1_ref,
+    wu_ref, bu_ref, wd_ref, bd_ref, g2_ref, s2_ref,
+    xc_o, gc_o, qkv_o, p_o, ctx_o, r1_o, n1_o, gelu_o, gelup_o, r2_o, back_o, col_o, pos_o,
+    xh, gh, xs, gs, xr, gr, hot, note_s, note_r, wq, wo, wu, wd, live_s,
+    xc_t, qkv_t, p_t, ctx_t, r1_t, n1_t, gelu_t, gelup_t, r2_t, bo_c, back_t, gc_t, col_t, pos_t,
+    load_sem, note_ss, note_rs, x_ss, x_rs, g_ss, g_rs, own_sem, out_sem, last_sem,
+):
+    rows, width = xh.shape
+    ffw = wu.shape[1]
+    blocks = rows // BLK
+    grp = lax.axis_index("grp")
+    me = lax.axis_index("tok")
+    order = peer_order(n_tok)
+
+    barrier = pltpu.get_barrier_semaphore()
+    for k in order:
+        pl.semaphore_signal(barrier, inc=1, device_id=(grp, me ^ k), device_id_type=MESH)
+
+    loads = [
+        pltpu.make_async_copy(src, dst, load_sem.at[i])
+        for i, (src, dst) in enumerate(
+            ((tok_ref, xh), (og_ref, gh), (wq_ref, wq), (wo_ref, wo), (wu_ref, wu), (wd_ref, wd))
+        )
+    ]
+    for copy in loads:
+        copy.start()
+
+    slots = slots_ref[...][None, :]
+    dest = jnp.right_shift(slots, rows.bit_length() - 1)
+    within = jnp.bitwise_and(slots, rows - 1)
+    lanes = lax.broadcasted_iota(jnp.int32, (1, rows), 1)
+    dest_hot = lax.broadcasted_iota(jnp.int32, (16, rows), 0) == dest
+    dest_hot = dest_hot.astype(f32)
+    before = lax.broadcasted_iota(jnp.int32, (BLK, rows), 1)
+    rank = jnp.zeros((16, rows), f32)
+    for b in range(blocks):
+        earlier = lax.broadcasted_iota(jnp.int32, (BLK, rows), 0) + b * BLK < before
+        rank += dot32(
+            dest_hot[:, b * BLK : (b + 1) * BLK].astype(bf16), earlier.astype(f32).astype(bf16)
+        )
+    rank = jnp.sum(rank * dest_hot, axis=0, keepdims=True).astype(jnp.int32)
+    pos = dest * per + rank
+    pos_t[...] = jnp.broadcast_to(pos, (8, rows))
+    start = jnp.int32(0)
+    position = lanes + me * rows
+    usable = jnp.zeros((1, rows), jnp.int32)
+    for i in range(docs_ref.shape[1]):
+        length = docs_ref[0, i]
+        inside = (position >= start) & (position < start + length)
+        usable = jnp.where(inside, 1, usable)
+        start = start + jnp.bitwise_and(length + (CLU - 1), -CLU)
+    for b in range(blocks):
+        spot = lax.broadcasted_iota(jnp.int32, (BLK, rows), 0) + b * BLK
+        hot[b * BLK : (b + 1) * BLK, :] = (spot == pos).astype(f32).astype(bf16)
+    kind = lax.broadcasted_iota(jnp.int32, (16, rows), 0)
+    notes = jnp.where(
+        kind == 0,
+        jnp.right_shift(within, 5),
+        jnp.where(kind == 1, jnp.bitwise_and(within, 31), jnp.where(kind == 2, usable, 0)),
+    )
+    notes = dot_rows(notes.astype(f32).astype(bf16), hot[...]).astype(bf16)
+    for d in range(n_tok):
+        note_s[d] = notes[:, d * per : (d + 1) * per]
+
+    def note_copy(k):
+        return pltpu.make_async_remote_copy(
+            src_ref=note_s.at[me ^ k], dst_ref=note_r.at[me], send_sem=note_ss.at[k],
+            recv_sem=note_rs.at[k], device_id=(grp, me ^ k), device_id_type=MESH,
+        )
+
+    def row_copy(src, dst, ss, rs, k):
+        return pltpu.make_async_remote_copy(
+            src_ref=src.at[pl.ds(pl.multiple_of((me ^ k) * per, per), per)],
+            dst_ref=dst.at[pl.ds(pl.multiple_of(me * per, per), per)],
+            send_sem=ss.at[k], recv_sem=rs.at[k], device_id=(grp, me ^ k), device_id_type=MESH,
+        )
+
+    pl.semaphore_wait(barrier, n_tok - 1)
+    for k in order:
+        note_copy(k).start()
+    loads[0].wait()
+    for b in range(blocks):
+        sl = pl.ds(b * BLK, BLK)
+        xs[sl, :] = dot32(hot[sl, :], xh[...]).astype(bf16)
+    for k in order:
+        row_copy(xs, xr, x_ss, x_rs, k).start()
+    mine = pl.ds(pl.multiple_of(me * per, per), per)
+    own_x = pltpu.make_async_copy(xs.at[mine], xr.at[mine], own_sem.at[0])
+    own_x.start()
+    own_note = pltpu.make_async_copy(note_s.at[me], note_r.at[me], own_sem.at[1])
+    own_note.start()
+    loads[1].wait()
+    for b in range(blocks):
+        sl = pl.ds(b * BLK, BLK)
+        gs[sl, :] = dot32(hot[sl, :], gh[...]).astype(bf16)
+    own_g = pltpu.make_async_copy(gs.at[mine], gr.at[mine], own_sem.at[2])
+    own_g.start()
+
+    own_note.wait()
+    for k in order:
+        note_copy(k).wait_recv()
+    got = jnp.concatenate([note_r[d] for d in range(n_tok)], axis=1)
+    got32 = got.astype(f32)
+    slot_row = got32[0:1, :] * 32.0 + got32[1:2, :]
+    col_t[...] = column_of(slot_row)
+    slot_row = slot_row.astype(jnp.int32)
+    for b in range(blocks):
+        spot = lax.broadcasted_iota(jnp.int32, (BLK, rows), 0) + b * BLK
+        hot[b * BLK : (b + 1) * BLK, :] = (spot == slot_row).astype(f32).astype(bf16)
+    live_s[...] = dot_rows(got, hot[...])
+
+    own_x.wait()
+    for k in order:
+        row_copy(xs, xr, x_ss, x_rs, k).wait_send()
+    for k in order:
+        row_copy(gs, gr, g_ss, g_rs, k).start()
+    for k in order:
+        row_copy(xs, xr, x_ss, x_rs, k).wait_recv()
+    for copy in loads[2:]:
+        copy.wait()
+
+    halves = lane_halves(2 * width // H)
+    pair_width = 2 * width // H
+    scale = (width // H) ** (-0.5)
+    outs = (
+        (xc_t, xc_o, BLK), (qkv_t, qkv_o, BLK), (p_t, p_o, BLK * H), (ctx_t, ctx_o, BLK), (r1_t, r1_o, BLK),
+        (n1_t, n1_o, BLK), (gelu_t, gelu_o, BLK), (gelup_t, gelup_o, BLK), (r2_t, r2_o, BLK),
+    )
+
+    def out_copy(i, b, slot):
+        tile, whole, count = outs[i]
+        return pltpu.make_async_copy(
+            tile.at[slot], whole.at[pl.ds(pl.multiple_of(b * count, count), count)], out_sem.at[slot, i]
+        )
+
+    def block(b, carry):
+        slot = lax.rem(b, 2)
+        sl = pl.ds(pl.multiple_of(b * BLK, BLK), BLK)
+
+        @pl.when(b >= 2)
+        def _():
+            for i in range(len(outs)):
+                out_copy(i, b - 2, slot).wait()
+
+        x = dot32(hot[sl, :], xr[...]).astype(bf16)
+        xc_t[slot] = x
+        for part, bias in ((0, row_of(bq_ref)), (1, None), (2, row_of(bv_ref))):
+            got_part = dot32(x, wq[:, part * width : (part + 1) * width])
+            if bias is not None:
+                got_part = got_part + bias
+            qkv_t[slot, :, part * width : (part + 1) * width] = got_part.astype(bf16)
+        for c in range(BLK // CLU):
+            at = pl.multiple_of(b * BLK + c * CLU, CLU)
+            live = live_s[2:3, pl.ds(at, CLU)] > 0.5
+            crow = pl.ds(c * CLU, CLU)
+            for p in range(H // 2):
+                cols = [pl.ds(part * width + p * pair_width, pair_width) for part in range(3)]
+                q2 = qkv_t[slot, crow, cols[0]]
+                k2 = qkv_t[slot, crow, cols[1]]
+                v2 = qkv_t[slot, crow, cols[2]]
+                scores = dot_rows(stack_heads(q2, halves), k2) * scale
+                scores = jnp.where(live, scores, masked_score)
+                expo = jnp.exp(scores - jnp.max(scores, axis=-1, keepdims=True))
+                weights = (expo / jnp.sum(expo, axis=-1, keepdims=True)).astype(bf16)
+                p_t[slot, pl.ds((c * H + 2 * p) * CLU, 2 * CLU), :] = weights
+                context = dot32(side_by_side(weights), stack_heads(v2, halves))
+                ctx_t[slot, crow, pl.ds(p * pair_width, pair_width)] = context.astype(bf16)
+        resid1 = x.astype(f32) + (dot32(ctx_t[slot], wo[...]) + row_of(bo_ref))
+        r1_t[slot] = resid1
+        hat1, _ = norm_parts(resid1)
+        normed1 = hat1 * row_of(g1_ref) + row_of(s1_ref)
+        low1 = normed1.astype(bf16)
+        n1_t[slot] = low1
+        down = None
+        step = width
+        for j in range(ffw // step):
+            cs = pl.ds(j * step, step)
+            up = dot32(low1, wu[:, cs]) + bu_ref[cs].astype(f32)[None, :]
+            phi = 0.5 * (1.0 + lax.erf(up * 0.7071067811865476))
+            slope = phi + up * jnp.exp(up * up * -0.5) * 0.3989422804014327
+            act = (up * phi).astype(bf16)
+            gelu_t[slot, :, cs] = act
+            gelup_t[slot, :, cs] = slope.astype(bf16)
+            term = dot32(act, wd[cs, :])
+            down = term if down is None else down + term
+        resid2 = normed1 + (down + row_of(bd_ref))
+        r2_t[slot] = resid2
+        hat2, _ = norm_parts(resid2)
+        bo_c[sl, :] = (hat2 * row_of(g2_ref) + row_of(s2_ref)).astype(bf16)
+        for i in range(len(outs)):
+            out_copy(i, b, slot).start()
+        return carry
+
+    lax.fori_loop(0, blocks, block, 0)
+
+    col_out = pltpu.make_async_copy(col_t, col_o, last_sem.at[0])
+    col_out.start()
+    pos_out = pltpu.make_async_copy(pos_t, pos_o, last_sem.at[1])
+    pos_out.start()
+    for b in range(blocks):
+        sl = pl.ds(b * BLK, BLK)
+        back_t[sl, :] = dot32(hot_from_column(col_t[sl, :], rows), bo_c[...]).astype(bf16)
+    back_out = pltpu.make_async_copy(back_t, back_o, last_sem.at[2])
+    back_out.start()
+    own_g.wait()
+    for k in order:
+        row_copy(gs, gr, g_ss, g_rs, k).wait_recv()
+    for b in range(blocks):
+        sl = pl.ds(b * BLK, BLK)
+        gc_t[sl, :] = dot32(hot[sl, :], gr[...]).astype(bf16)
+    gc_out = pltpu.make_async_copy(gc_t, gc_o, last_sem.at[3])
+    gc_out.start()
+    for k in order:
+        note_copy(k).wait_send()
+        row_copy(gs, gr, g_ss, g_rs, k).wait_send()
+    for b in range(max(blocks - 2, 0), blocks):
+        for i in range(len(outs)):
+            out_copy(i, b, b % 2).wait()
+    col_out.wait()
+    pos_out.wait()
+    back_out.wait()
+    gc_out.wait()
+
+
+def forward(n_tok, tokens_in, w_qkv, b_query, b_value, w_out, b_out, norm1_gain, norm1_shift,
+            w_up, b_up, w_down, b_down, norm2_gain, norm2_shift, out_grad, doc_lengths, cluster_slots):
+    rows, width = tokens_in.shape
+    ffw = w_up.shape[1]
+    per = rows // n_tok
+    vm = pl.BlockSpec(memory_space=pltpu.VMEM)
+    sm = pl.BlockSpec(memory_space=pltpu.SMEM)
+    hb = pl.BlockSpec(memory_space=pl.ANY)
+    out_shape = [
+        ((rows, width), bf16), ((rows, width), bf16), ((rows, 3 * width), bf16), ((rows * H, CLU), bf16),
+        ((rows, width), bf16), ((rows, width), f32), ((rows, width), bf16), ((rows, ffw), bf16),
+        ((rows, ffw), bf16), ((rows, width), f32), ((rows, width), bf16), ((rows, 128), f32),
+        ((8, rows), jnp.int32),
+    ]
+    vmem = pltpu.VMEM
+    dma = pltpu.SemaphoreType.DMA
+    scratch = (
+        [vmem((rows, width), bf16)] * 6
+        + [vmem((rows, rows), bf16), vmem((n_tok, 16, per), bf16), vmem((n_tok, 16, per), bf16)]
+        + [vmem(w_qkv.shape, bf16), vmem(w_out.shape, bf16), vmem(w_up.shape, bf16), vmem(w_down.shape, bf16)]
+        + [vmem((16, rows), f32)]
+        + [
+            vmem((2, BLK, width), bf16), vmem((2, BLK, 3 * width), bf16), vmem((2, BLK * H, CLU), bf16),
+            vmem((2, BLK, width), bf16), vmem((2, BLK, width), f32), vmem((2, BLK, width), bf16),
+            vmem((2, BLK, ffw), bf16), vmem((2, BLK, ffw), bf16), vmem((2, BLK, width), f32),
+            vmem((rows, width), bf16), vmem((rows, width), bf16), vmem((rows, width), bf16),
+            vmem((rows, 128), f32), vmem((8, rows), jnp.int32),
+        ]
+        + [dma((6,))] + [dma((n_tok,))] * 6 + [dma((3,)), dma((2, 9)), dma((4,))]
+    )
+    return pl.pallas_call(
+        functools.partial(forward_kernel, n_tok, per),
+        out_shape=[jax.ShapeDtypeStruct(s, d) for s, d in out_shape],
+        in_specs=[vm, sm, hb, hb, hb, vm, vm, hb, vm, vm, vm, hb, vm, hb, vm, vm, vm],
+        out_specs=[hb] * len(out_shape),
+        scratch_shapes=scratch,
+        compiler_params=pltpu.CompilerParams(
+            collective_id=0, has_side_effects=True, vmem_limit_bytes=60 * 2**20
+        ),
+        name="layer_forward",
+    )(cluster_slots, doc_lengths, tokens_in, out_grad, w_qkv, b_query, b_value, w_out, b_out, norm1_gain,
+      norm1_shift, w_up, b_up, w_down, b_down, norm2_gain, norm2_shift)
 
 
 def gelu_exact(values):
@@ -28,10 +362,6 @@
         position[:, None] < (starts + lengths_row)[None, :]
     )
     return jnp.any(inside, axis=1)
-
-
-def dot32(a, b):
-    return jnp.dot(a, b, preferred_element_type=jnp.float32)
 
 
 def move(one_hot, rows):
@@ -185,7 +515,119 @@
     )
 
 
+def norm_rows(values, scales, shifts):
+    centre = values - jnp.mean(values, axis=-1, keepdims=True)
+    spread = jnp.mean(centre * centre, axis=-1, keepdims=True)
+    return centre * lax.rsqrt(spread + eps) * scales + shifts
+
+
+def per_device_fast(
+    tokens_in, w_qkv, b_query, b_value, w_out, b_out, norm1_gain, norm1_shift,
+    w_up, b_up, w_down, b_down, norm2_gain, norm2_shift, out_grad, doc_lengths, cluster_slots,
+):
+    tok_dev, width = tokens_in.shape
+    head_size = width // H
+    clusters = tok_dev // CLU
+    n_tok = lax.axis_size("tok")
+    my_index = lax.axis_index("tok")
+    scale = head_size ** (-0.5)
+    (x, g, qkv, weights, context, resid1, normed1_low, gelu_low, gelup, resid2, back, col, pos) = forward(
+        n_tok, tokens_in, w_qkv, b_query, b_value, w_out, b_out, norm1_gain, norm1_shift,
+        w_up, b_up, w_down, b_down, norm2_gain, norm2_shift, out_grad, doc_lengths, cluster_slots)
+    send_hot = (jnp.arange(tok_dev)[:, None] == pos[0][None, :]).astype(bf16)
+    place_hot = (jnp.arange(tok_dev, dtype=f32)[:, None] == col[:, 0][None, :]).astype(bf16)
+    block_out = move_back(send_hot, exchange(back))
+    _, norm1_back = jax.vjp(norm_rows, resid1, norm1_gain.astype(f32), norm1_shift.astype(f32))
+    _, norm2_back = jax.vjp(norm_rows, resid2, norm2_gain.astype(f32), norm2_shift.astype(f32))
+    grad_resid2, grad_gain2, grad_shift2 = norm2_back(g.astype(f32))
+    grad_down = grad_resid2.astype(jnp.bfloat16)
+    grad_b_down = jnp.sum(grad_down.astype(f32), axis=0)
+    grad_w_down = jnp.einsum("nf,nd->fd", gelu_low, grad_down, preferred_element_type=f32)
+    grad_gelu = jnp.einsum("nd,fd->nf", grad_down, w_down, preferred_element_type=f32)
+    grad_up = (grad_gelu * gelup.astype(f32)).astype(jnp.bfloat16)
+    grad_b_up = jnp.sum(grad_up.astype(f32), axis=0)
+    grad_w_up = jnp.einsum("nd,nf->df", normed1_low, grad_up, preferred_element_type=f32)
+    grad_normed1 = grad_resid2 + jnp.einsum(
+        "nf,df->nd", grad_up, w_up, preferred_element_type=f32
+    )
+    grad_resid1, grad_gain1, grad_shift1 = norm1_back(grad_normed1)
+    grad_attn = grad_resid1.astype(jnp.bfloat16)
+    grad_b_out = jnp.sum(grad_attn.astype(f32), axis=0)
+    grad_w_out = jnp.einsum("nd,ne->de", context, grad_attn, preferred_element_type=f32)
+    grad_context = jnp.einsum("ne,de->nd", grad_attn, w_out, preferred_element_type=f32)
+    grad_context = grad_context.astype(jnp.bfloat16).reshape(clusters, CLU, H, head_size)
+
+    packed = qkv.reshape(clusters, CLU, 3, H, head_size)
+    query, keys, value = packed[:, :, 0], packed[:, :, 1], packed[:, :, 2]
+    weights = weights.reshape(clusters, H, CLU, CLU)
+    probs = weights.astype(f32)
+    grad_probs = jnp.einsum("bqhd,bkhd->bhqk", grad_context, value, preferred_element_type=f32)
+    row_dot = jnp.sum(grad_probs * probs, axis=-1, keepdims=True)
+    grad_scores = (probs * (grad_probs - row_dot)).astype(jnp.bfloat16)
+    grad_q = jnp.einsum("bhqk,bkhd->bqhd", grad_scores, keys, preferred_element_type=f32) * scale
+    grad_k = jnp.einsum("bhqk,bqhd->bkhd", grad_scores, query, preferred_element_type=f32) * scale
+    grad_v = jnp.einsum("bhqk,bqhd->bkhd", weights, grad_context, preferred_element_type=f32)
+    grad_qkv = jnp.stack([grad_q, grad_k, grad_v], axis=2).astype(jnp.bfloat16)
+    grad_qkv = grad_qkv.reshape(tok_dev, 3 * width)
+    grad_total = grad_resid1 + jnp.einsum(
+        "ne,de->nd", grad_qkv, w_qkv, preferred_element_type=f32
+    )
+    back_got = exchange(move_back(place_hot, grad_total.astype(jnp.bfloat16)))
+    grad_tokens = move_back(send_hot, back_got)
+    grad_w_qkv = jnp.einsum("nd,ne->de", x, grad_qkv, preferred_element_type=f32)
+    grad_qkv_sum = jnp.sum(grad_qkv.astype(f32), axis=0)
+
+    low = jnp.bfloat16
+    wide = jnp.concatenate(
+        [
+            grad_w_qkv.astype(low), grad_w_out.astype(low), grad_w_up.astype(low),
+            grad_w_down.astype(low).reshape(width, -1),
+        ],
+        axis=1,
+    )
+    narrow = jnp.concatenate(
+        [
+            member.reshape(n_tok, -1)
+            for member in (
+                grad_qkv_sum[:width], grad_qkv_sum[2 * width :], grad_b_out, grad_gain1,
+                grad_shift1, grad_b_down, grad_gain2, grad_shift2, grad_b_up,
+            )
+        ],
+        axis=1,
+    )
+    share = lax.psum_scatter(wide, "tok", scatter_dimension=0, tiled=True)
+    share = lax.psum(share, "grp").astype(f32)
+    narrow = lax.psum(narrow, ("grp", "tok"))
+    mine = lax.dynamic_index_in_dim(narrow, my_index, 0, keepdims=False)
+    step = width // n_tok
+    parts = [mine[i * step : (i + 1) * step] for i in range(8)] + [mine[8 * step :]]
+    ffw = w_up.shape[1]
+    return (
+        block_out,
+        grad_tokens,
+        share[:, : 3 * width],
+        parts[0],
+        parts[1],
+        share[:, 3 * width : 4 * width],
+        parts[2],
+        parts[3],
+        parts[4],
+        share[:, 4 * width : 4 * width + ffw],
+        parts[8],
+        share[:, 4 * width + ffw :].reshape(ffw // n_tok, width),
+        parts[5],
+        parts[6],
+        parts[7],
+    )
+
+
 def solution(mesh):
+    n_tok = mesh.shape["tok"]
+
+    def body(*args):
+        even = (args[0].shape[0] // n_tok) % 128 == 0 and n_tok & (n_tok - 1) == 0
+        return (per_device_fast if even and mesh.shape["grp"] == 4 else per_device)(*args)
+
     rows = P(("grp", "tok"), None)
     in_specs = (rows,) + (P(),) * 13 + (rows, P("grp", None), P(("grp", "tok")))
     shares = (
@@ -193,5 +635,5 @@
         P("tok", None), P("tok"), P("tok", None), P("tok"), P("tok"), P("tok"),
     )
     return jax.shard_map(
-        per_device, mesh=mesh, in_specs=in_specs, out_specs=(rows, rows) + shares, check_vma=False
-    )
+        body, mesh=mesh, in_specs=in_specs, out_specs=(rows, rows) + shares, check_vma=False
+    )

time: 588 us -> 513 us (0.87)
  matrix products: 167 us -> 66.8 us
  Pallas kernels: 0 us -> 92.3 us
  other arithmetic: 46.7 us -> 26.2 us
  local copies, waits for them, and re-layouts: 72.4 us -> 52.5 us
  starting transfers between devices: 24.7 us -> 8.28 us
  waiting for transfers between devices: 199 us -> 187 us
    dot_general x21 -> x11, matrix products: 142 us -> 45.3 us  [the longest x1 8.77 us: per_device_fast(): jnp.einsum('nd,fd->nf', grad_down, w_down, preferred_element_type=f32)]
    pallas_call x0 -> x1, Pallas kernels: none -> 92.3 us  [forward(): pl.pallas_call(functools.partial(forward_kernel, n_tok, per), out_shape=[...]
    all_to_all x5 -> x2, waiting for transfers between devices: 83.5 us -> 47.4 us  [exchange(): return lax.all_to_all(rows, 'tok', split_axis=0, concat_axis=0, tiled=True)]
    all_to_all x5 -> x2, starting transfers between devices: 24.4 us -> 8.2 us  [exchange(): return lax.all_to_all(rows, 'tok', split_axis=0, concat_axis=0, tiled=True)]
    psum x1, waiting for transfers between devices: 2.31 us -> 15.8 us  [per_device_fast(): share = lax.psum(share, 'grp').astype(f32)]
    reduce_scatter x1, waiting for transfers between devices: 113 us -> 124 us  [per_device_fast(): share = lax.psum_scatter(wide, 'tok', scatter_dimension=0, tiled=True)]
    convert_element_type x5 -> x3, local copies, waits for them, and re-layouts: 22.3 us -> 11.5 us  [the longest x1 9.28 us: per_device_fast(): grad_qkv = jnp.stack([grad_q, grad_k, grad_v], axis=2).astype(jnp.bfloat16)]
    convert_element_type x11 -> x3, other arithmetic: 12.8 us -> 2.69 us  [the longest x1 1.32 us: per_device_fast(): grad_scores = (probs * (grad_probs - row_dot)).astype(jnp.bfloat16)]
  transfers between devices with their start and end apart: 7 -> 4, of which waited for: 5 -> 3; matrix products, arithmetic and copies ran while one was open for 22% -> 5% of each run, Pallas kernels for 0% -> 0%
where the time goes in v2:
time: 513 us; the launch traced here: 504 us
  waiting for transfers between devices  187 us (36%)
  Pallas kernels  92.3 us (18%)
  matrix products  66.8 us (13%)
  blocking collectives  55 us (11%)
  local copies, waits for them, and re-layouts  52.5 us (10%)
  other arithmetic  26.2 us (5%)
  between operations  15.1 us (3%)
  starting transfers between devices  8.28 us (2%)
    reduce_scatter x1, waiting for transfers between devices, per_device_fast(): share = lax.psum_scatter(wide, 'tok', scatter_dimension=0, tiled=True)  124 us
    pallas_call x1, Pallas kernels, forward(): pl.pallas_call(functools.partial(forward_kernel, n_tok, per), out_shape=[...  92.3 us
    psum x1, blocking collectives, per_device_fast(): narrow = lax.psum(narrow, ('grp', 'tok'))  55 us
    all_to_all x2, waiting for transfers between devices, exchange(): return lax.all_to_all(rows, 'tok', split_axis=0, concat_axis=0, tiled=True)  47.4 us
    dot_general x3, matrix products, move_back(): jnp.einsum('pi,pd->id', one_hot, rows, preferred_element_type=jnp.float32)  21.5 us
    psum x1, waiting for transfers between devices, per_device_fast(): share = lax.psum(share, 'grp').astype(f32)  15.8 us
    unnamed x50, local copies, waits for them, and re-layouts  12.2 us
  transfers between devices with their start and end apart: 4, of which 3 were waited for; matrix products, arithmetic and copies ran while one was open for 5% of the time, Pallas kernels for 0%

profile of v2, /device:TPU:0, one launch (start us, length us, event | category | flops | bytes accessed | tf_op | source)
XLA Modules:
  0.0 503.7 jit_solution(1301557237832619498)
XLA Ops:
  7.2 0.7 convert_element_type.86
  7.9 0.7 convert_element_type.82
  8.6 92.3 %layer_forward.1 = (bf16[1024,768]{1,0:T(8,128)(2,1)}, bf16[1024,768]{1,0:T(8,128)(2,1)}, bf16[1024,2304]{1,0:T(8,128)(2,1)}, bf16[12288,128]{1,0:T(8,128)(2,1)}...) custom-call(s32[1024]{0:T(1024)} %slots_ref.1, ...), custom_call_target="tpu_custom_call" | custom-call | tf_op jit(solution)/shard_map/layer_forward/pallas_call | solution.py:339
  101.0 2.3 reduce_sum.148
  103.2 0.6 copy-done
  103.8 0.5 multiply_reduce_fusion.3
  104.3 2.1 reduce_sum.155
  106.4 3.6 fusion.13
  110.0 1.4 fusion.30
  111.5 1.7 copy-done.3
  113.2 0.3 convert_reduce_fusion.3
  113.6 0.2 slice-done.7
  113.7 6.9 %convolution_convert_fusion = bf16[3072,768]{1,0:T(8,128)(2,1)} fusion(bf16[1024,3072]{1,0:T(8,128)(2,1)S(1)} %bitcast.108, bf16[1024,768]{1,0:T(8,128)(2,1)S(1)} %get-tuple-element.48), kind=kOutput, calls=%fused_computation.9 | convolution fusion | flops 4834197504 | bytes 12582912 | tf_op jit(solution)/shard_map/nf,nd->fd/dot_general | solution.py:545
  120.7 8.5 %reshape.164 = bf16[768,3072]{1,0:T(8,128)(2,1)} reshape(bf16[3072,768]{1,0:T(8,128)(2,1)} %convolution_convert_fusion) | data formatting | bytes 9437184 | tf_op jit(solution)/shard_map/reshape | solution.py:584
  129.2 8.8 %convert_reduce_fusion = (f32[3072]{0:T(1024)S(1)}, bf16[1024,3072]{1,0:T(8,128)(2,1)S(1)}) fusion(bf16[1024,3072]{1,0:T(8,128)(2,1)} %get-tuple-element.33, bf16[1024,768]{1,0:T(8,128)(2,1)S(1)} %get-tuple-element.48, bf16[3072,768]{1,0:T(8,128)(2,1)} %wd_ref.1), kind=kOutput, calls=%fused_computation.1 | convolution fusion | flops 4847563776 | bytes 18886656 | tf_op jit(solution)/shard_map/nd,fd->nf/dot_general | solution.py:546
  138.0 7.3 %convolution_convert_fusion.1 = bf16[768,3072]{1,0:T(8,128)(2,1)} fusion(bf16[1024,768]{1,0:T(8,128)(2,1)S(1)} %copy-done.15, bf16[1024,3072]{1,0:T(8,128)(2,1)S(1)} %get-tuple-element.76), kind=kOutput, calls=%fused_computation.10 | convolution fusion | flops 4834197504 | bytes 12582912 | tf_op jit(solution)/shard_map/nd,nf->df/dot_general | solution.py:549
  145.3 6.0 %multiply_reduce_fusion = (f32[768]{0:T(1024)S(1)}, f32[1024]{0:T(1024)S(1)}, f32[768]{0:T(1024)S(1)}, f32[1024,768]{1,0:T(8,128)S(1)}) fusion(f32[1024,768]{1,0:T(8,128)S(1)} %copy-done.1, f32[1024]{0:T(1024)S(1)} %fusion.28, f32[1024]{0:T(1024)S(1)} %broadcast_multiply_fusion, f32[768]{0:T(1024)S(1)} %convert_element_type.86, ...), kind=kOutput, calls=%fused_computation.32 | convolution fusion | flops 4839699456 | bytes 20472832 | tf_op jit(solution)/shard_map/nf,df->nd/dot_general | solution.py:550
  151.4 1.5 fusion.29
  152.9 0.3 convert_reduce_fusion.4
  153.2 1.8 copy-done.12
  155.0 1.4 convolution_convert_fusion.3
  156.5 1.5 convolution_convert_fusion.4
  158.0 1.5 copy.52
  159.4 0.7 copy.44
  160.2 1.6 copy.59
  161.8 3.7 copy.43
  165.4 4.5 convolution_bitcast_fusion
  169.9 6.7 %copy.41 = bf16[1024,2304]{0,1:T(8,128)(2,1)} copy(bf16[1024,2304]{1,0:T(8,128)(2,1)} %get-tuple-element.35) | data formatting | bytes 9437184 | tf_op jit(solution)/shard_map/layer_forward/pallas_call | solution.py:339
  176.6 3.6 copy.58
  180.1 0.4 fusion.31
  180.5 1.0 copy-done.2
  181.5 1.5 fusion
  183.1 1.3 fusion.1
  184.4 2.3 multiply_bitcast_fusion
  186.7 1.0 multiply_bitcast_fusion.1
  187.6 0.4 copy-done.9
  188.1 1.9 convert_reduce_fusion.1
  190.0 9.3 %copy.51 = bf16[8,128,3,12,64]{1,0,4,3,2:T(8,128)(2,1)S(1)} copy(bf16[8,128,3,12,64]{1,4,3,0,2:T(8,128)(2,1)S(1)} %get-tuple-element.52) | data formatting | bytes 9437184 | tf_op jit(solution)/shard_map/convert_element_type | solution.py:570
  199.4 4.1 convolution_convert_fusion.2
  203.6 1.3 slice-done.3
  204.8 9.6 %pad_maximum_fusion = bf16[768,9216]{1,0:T(8,128)(2,1)} fusion(bf16[768,3072]{1,0:T(8,128)(2,1)S(1)} %bitcast.88, bf16[768,3072]{1,0:T(8,128)(2,1)S(1)} %bitcast.97, bf16[768,768]{1,0:T(8,128)(2,1)S(1)} %copy-done.10, bf16[768,2304]{1,0:T(8,128)(2,1)S(1)} %convolution_convert_fusion.2), kind=kLoop, calls=%fused_computation | loop fusion | flops 56623104 | bytes 28311552 | tf_op jit(solution)/shard_map/concatenate | solution.py:581
  214.5 4.6 all-to-all-start
  219.0 1.2 slice_reduce_fusion
  220.3 13.3 %fusion.19 = bf16[1024,768]{1,0:T(8,128)(2,1)} fusion(f32[1024]{0:T(1024)S(1)} %slice_reduce_fusion, f32[1024,768]{1,0:T(8,128)S(1)} %copy-done.6, bf16[768,2304]{1,0:T(8,128)(2,1)} %wq_ref.1, bf16[288,8,8,128]{3,2,1,0:T(8,128)(2,1)} %bitcast.99, f32[1024]{0:T(1024)S(1)} %negate_multiply_fusion), kind=kOutput, calls=%fused_computation.47 | convolution fusion | flops 5238685696 | bytes 12984320 | tf_op jit(solution)/shard_map/pi,pd->id/dot_general | solution.py:372
  233.6 47.4 %all-to-all-done = bf16[8,128,768]{2,1,0:T(8,128)(2,1)} async-done(((bf16[8,128,768]{2,1,0:T(8,128)(2,1)}), bf16[8,128,768]{2,1,0:T(8,128)(2,1)}, u32[]{:S(2)}, u32[]{:S(2)}) %all-to-all-start) | async-done | bytes 1572896 | tf_op jit(solution)/shard_map/all_to_all | solution.py:377
  281.0 3.6 all-to-all-start.1
  284.7 124.3 %reduce-scatter.2.cloned.1.call-done = bf16[96,9216]{1,0:T(8,128)(2,1)} async-done(((bf16[768,9216]{1,0:T(8,128)(2,1)}), bf16[96,9216]{1,0:T(8,128)(2,1)}) %reduce-scatter.2.cloned.1.call-update) | async-done | bytes 1769488 | tf_op jit(solution)/shard_map/reduce_scatter | solution.py:598
  409.0 0.8 slice.97
  409.8 0.1 reshape.169
  409.9 0.1 reshape.170
  409.9 0.1 reshape.168
  410.0 0.1 reshape.166
  410.2 0.1 slice.106
  410.4 0.1 concatenate.7
  410.5 55.0 %psum.15 = f32[8,1152]{1,0:T(8,128)S(1)} all-reduce(f32[8,1152]{1,0:T(8,128)S(1)} %concatenate.7), channel_id=1, replica_groups=mesh['grp'=4,'tok'=8] {'grp','tok'}, use_global_device_ids=true, to_apply=%region_19.0 | all-reduce | flops 9216 | bytes 73728 | tf_op jit(solution)/shard_map/psum | solution.py:600
  465.4 0.7 dynamic-slice_reduce_fusion
  466.1 0.6 dynamic-slice_bitcast_fusion
  466.7 4.8 fusion.20
  471.5 3.4 fusion.21
  474.9 15.8 %all-reduce.2.cloned.1.call-done = bf16[96,9216]{1,0:T(8,128)(2,1)} async-done(((bf16[96,9216]{1,0:T(8,128)(2,1)}), bf16[96,9216]{1,0:T(8,128)(2,1)}) %all-reduce.2.cloned.1.call-update) | async-done | bytes 1769488 | tf_op jit(solution)/shard_map/psum | solution.py:599
  490.7 2.6 fusion.32
  493.3 1.3 reshape.172
  494.7 0.7 slice.134
  495.4 1.0 slice.131
  (63 shorter events, 0.5 us)
Async XLA Ops:
  7.2 401.8 %reduce-scatter.2.cloned.1.call-start = ((), (), s32[]{:S(2)}) async-start(), calls=%async_computation.3 | async-start | bytes 15925248 | tf_op jit(solution)/shard_map/reduce_scatter | solution.py:598
  100.9 2.8 copy-start
  106.4 3.6 copy-start.8
  110.0 3.6 slice-start.6
  110.0 3.7 slice-start.7
  111.5 1.8 copy-start.3
  120.7 24.6 %slice-start.4 = ((s8[4718592]{0:T(1024)(128)(4,1)}), s8[524288]{0:T(1024)(128)(4,1)S(1)}, s32[]{:S(2)}) async-start(s8[4718592]{0:T(1024)(128)(4,1)} %bitcast.100), calls=%async_computation.9 | async-start | bytes 1048576
  129.2 8.8 %copy-start.15 = (bf16[1024,768]{1,0:T(8,128)(2,1)S(1)}, bf16[1024,768]{1,0:T(8,128)(2,1)}, u32[]{:S(2)}) copy-start(bf16[1024,768]{1,0:T(8,128)(2,1)} %get-tuple-element.39) | copy-start | bytes 4718596
  129.2 16.1 %slice-start.5 = ((s8[4718592]{0:T(1024)(128)(4,1)}), s8[4194304]{0:T(1024)(128)(4,1)S(1)}, s32[]{:S(2)}) async-start(s8[4718592]{0:T(1024)(128)(4,1)} %bitcast.100), calls=%async_computation.10 | async-start | bytes 8388608
  138.0 7.3 %copy-start.1 = (f32[1024,768]{1,0:T(8,128)S(1)}, f32[1024,768]{1,0:T(8,128)}, u32[]{:S(2)}) copy-start(f32[1024,768]{1,0:T(8,128)} %get-tuple-element.34) | copy-start | bytes 9437188
  138.0 7.3 %copy-start.4 = (f32[1024,768]{1,0:T(8,128)S(1)}, f32[1024,768]{1,0:T(8,128)}, u32[]{:S(2)}) copy-start(f32[1024,768]{1,0:T(8,128)} %copy-done.3) | copy-start | bytes 9437188
  152.9 3.6 copy-start.5
  152.9 2.1 copy-start.12
  155.0 1.4 copy-start.14
  180.1 1.4 copy-start.2
  186.7 1.4 copy-start.9
  190.0 9.3 %copy-start.13 = (bf16[1024,768]{1,0:T(8,128)(2,1)S(1)}, bf16[1024,768]{1,0:T(8,128)(2,1)}, u32[]{:S(2)}) copy-start(bf16[1024,768]{1,0:T(8,128)(2,1)} %get-tuple-element.37) | copy-start | bytes 4718596
  190.0 13.5 %slice-start = ((s8[4718592]{0:T(1024)(128)(4,1)}), s8[524288]{0:T(1024)(128)(4,1)S(1)}, s32[]{:S(2)}) async-start(s8[4718592]{0:T(1024)(128)(4,1)} %bitcast.87), calls=%async_computation.5 | async-start | bytes 1048576
  190.0 13.5 %slice-start.2 = ((s8[4718592]{0:T(1024)(128)(4,1)}), s8[524288]{0:T(1024)(128)(4,1)S(1)}, s32[]{:S(2)}) async-start(s8[4718592]{0:T(1024)(128)(4,1)} %bitcast.96), calls=%async_computation.7 | async-start | bytes 1048576
  199.3 4.2 copy-start.11
  199.3 4.2 slice-start.1
  199.4 4.2 copy-start.10
  199.4 5.5 %slice-start.3 = ((s8[4718592]{0:T(1024)(128)(4,1)}), s8[4194304]{0:T(1024)(128)(4,1)S(1)}, s32[]{:S(2)}) async-start(s8[4718592]{0:T(1024)(128)(4,1)} %bitcast.96), calls=%async_computation.8 | async-start | bytes 8388608
  214.5 5.8 %copy-start.6 = (f32[1024,768]{1,0:T(8,128)S(1)}, f32[1024,768]{1,0:T(8,128)}, u32[]{:S(2)}) copy-start(f32[1024,768]{1,0:T(8,128)} %copy-done.5) | copy-start | bytes 9437188
  214.5 66.5 %all-to-all-start = ((bf16[8,128,768]{2,1,0:T(8,128)(2,1)}), bf16[8,128,768]{2,1,0:T(8,128)(2,1)}, u32[]{:S(2)}, u32[]{:S(2)}) async-start(bf16[8,128,768]{2,1,0:T(8,128)(2,1)} %bitcast.102), calls=%async_computation | async-start | bytes 3145728 | tf_op jit(solution)/shard_map/all_to_all | solution.py:377
  281.0 190.5 %all-to-all-start.1 = ((bf16[8,128,768]{2,1,0:T(8,128)(2,1)}), bf16[8,128,768]{2,1,0:T(8,128)(2,1)S(1)}, u32[]{:S(2)}, u32[]{:S(2)}) async-start(bf16[8,128,768]{2,1,0:T(8,128)(2,1)} %bitcast.103), calls=%async_computation.1 | async-start | bytes 3145728 | tf_op jit(solution)/shard_map/all_to_all | solution.py:377
  284.7 206.0 %all-reduce.2.cloned.1.call-start = ((), (), s32[]{:S(2)}) async-start(), calls=%async_computation.4 | async-start | bytes 3538944 | tf_op jit(solution)/shard_map/psum | solution.py:599
  490.7 4.0 copy-start.7
Sparse Core Ops, SparseCore 0:
  214.6 194.3 reduce-scatter.1
  412.2 78.4 all-reduce.1
